TPU v7x, 256 devices: a whole 4x4x8 slice. The times are simulated.
256 devices in a mesh: lat: 16 (over x_lo, y, core), lon: 16 (over x_hi, z).
Axes of the slice: x: 4 (x_hi: 2, x_lo: 2; x = x_hi * 2 + x_lo), y: 4, z: 8, core: 2. Of those that a mesh axis runs over, the one named last changes fastest.
Arguments:
- state: float32 [512, 3600, 128], P('lat', 'lon'), may hold values from -6 to 6
- zonal_coef: float32 [512], P('lat'), may hold values from 0.02 to 0.2
- diffusivity: float32 [128], replicated, may hold values from 0.5 to 2
- coupling: float32 [128, 128], replicated, may hold values from -0.5 to 0.5
- filter_rows: int32 [192], replicated, may hold values from 0 to 511, as said below
- band_width: int32 [512], replicated, may hold values from 1 to 16
- table_index: int32 [512], replicated, may hold values from 0 to 15
- coef_table: float32 [16, 17], replicated, may hold values from -1.2 to 1.2
Outputs:
- updated: float32 [512, 3600, 128], P('lat', 'lon')
Inputs may be any that keep to these rules, and one draw needn't show every extreme that they name: `filter_rows`: 192 distinct rows in increasing order: every row less than 64 rows from either pole, and half of the rows from 64 to 128 rows from each pole.
All inputs are finite; a program needn't handle non-finite values.
Results may differ from a plain program's by a relative error of at most 0.00007.
Values sent between devices are 32-bit elements; how exact they have to be, the bound alone decides.
A program may use at most 128 MiB of HBM per device.

v0:
```python
import jax
import jax.numpy as jnp
from jax import lax
from jax.sharding import PartitionSpec as P

MAXB = 16


meridional_rate = 0.1


def extended_2(block, sides, width):
    for axis, dim in sides:
        count = lax.axis_size(axis)
        forward = [(i, i + 1) for i in range(count - 1)]
        forward.append((count - 1, 0))
        backward = [(target, source) for source, target in forward]
        low = lax.ppermute(
            lax.slice_in_dim(block, block.shape[dim] - width, None, axis=dim), axis, forward
        )
        high = lax.ppermute(lax.slice_in_dim(block, 0, width, axis=dim), axis, backward)
        block = jnp.concatenate([low, block, high], axis=dim)
    return block


def row_weights(rows, band_width, table_index, coef_table):
    select = rows[:, None] == jnp.arange(band_width.shape[0])[None, :]
    tables = jnp.sum(jnp.where(select, table_index[None, :], 0), axis=1)
    widths = jnp.sum(jnp.where(select, band_width[None, :], 0), axis=1)
    choose = (tables[:, None] == jnp.arange(coef_table.shape[0])[None, :]).astype(jnp.float32)
    picked = jnp.dot(
        choose, coef_table, precision=lax.Precision.HIGHEST, preferred_element_type=jnp.float32
    )
    reach = jnp.arange(coef_table.shape[1])[None, :] <= widths[:, None]
    return jnp.where(reach, picked, jnp.float32(0.0))


def band_taps(extended, weights, length):
    total = weights[:, 0, None, None] * extended[:, MAXB : MAXB + length]
    for step in range(1, MAXB + 1):
        before = extended[:, MAXB - step : MAXB - step + length]
        after = extended[:, MAXB + step : MAXB + step + length]
        total = total + weights[:, step, None, None] * (before + after)
    return total


def local(
    state, zonal_coef, diffusivity, coupling, filter_rows, band_width, table_index, coef_table
):
    rows, cols, chans = state.shape
    lat_count = lax.axis_size("lat")
    lat_pos = lax.axis_index("lat")
    padded = extended_2(state, (("lat", 0), ("lon", 1)), 1)
    keep = jnp.ones((rows + 2,), jnp.float32)
    keep = keep.at[0].set(jnp.where(lat_pos == 0, 0.0, 1.0))
    keep = keep.at[rows + 1].set(jnp.where(lat_pos == lat_count - 1, 0.0, 1.0))
    padded = padded * keep[:, None, None]
    inner = padded[1:-1, 1:-1]
    east = padded[1:-1, 2:]
    west = padded[1:-1, :-2]
    north = padded[2:, 1:-1]
    south = padded[:-2, 1:-1]
    tendency = zonal_coef[:, None, None] * (east + west - 2.0 * inner) + meridional_rate * (
        north + south - 2.0 * inner
    )
    stepped = inner + diffusivity[None, None, :] * tendency
    flat = stepped.reshape(-1, chans)
    coupled_wide = stepped + jnp.dot(
        flat, coupling, precision=lax.Precision.HIGHEST, preferred_element_type=jnp.float32
    ).reshape(stepped.shape)
    work_rows = lat_pos * rows + jnp.arange(rows, dtype=jnp.int32)
    weights = row_weights(work_rows, band_width, table_index, coef_table)
    listed = jnp.any(work_rows[:, None] == filter_rows[None, :], axis=1)
    extended = extended_2(coupled_wide, (("lon", 1),), MAXB)
    smooth = band_taps(extended, weights, cols)
    filtered = jnp.where(listed[:, None, None], smooth, coupled_wide)
    return filtered


def solution(mesh):
    return jax.shard_map(
        local,
        mesh=mesh,
        in_specs=(P("lat", "lon", None), P("lat"), P(), P(), P(), P(), P(), P()),
        out_specs=P("lat", "lon", None),
        check_vma=False,
    )
```

profile of v0, /device:TPU:2, one launch (start us, length us, event | category | flops | bytes accessed | tf_op | source)
XLA Modules:
  0.0 113.9 jit_solution(2008991738081968208)
XLA Ops:
  0.0 0.0 copy-start
  0.0 1.7 %fusion.97 = (f32[1,225,128]{2,0,1:T(1,128)S(1)}, f32[1,225,128]{2,0,1:T(1,128)S(1)}) fusion(f32[32,225,128]{2,0,1:T(8,128)} %param.12), kind=kLoop, calls=%fused_computation.187 | loop fusion | bytes 460800 | tf_op jit(solution)/shard_map/slice | solution.py:21
  1.7 0.1 collective-permute-start
  1.8 3.9 %collective-permute-start.1 = (f32[1,225,128]{2,1,0:T(8,128)S(1)}, f32[1,225,128]{2,1,0:T(8,128)S(1)}, u32[]{:S(2)}, u32[]{:S(2)}) collective-permute-start(f32[1,225,128]{2,1,0:T(8,128)S(1)} %copy.19), channel_id=1, source_target_pairs={{16,0},{32,16},{48,32},{64,48},{80,64},{96,80},{112,96},{128,112},... | collective-permute-start | bytes 345608 | tf_op jit(solution)/shard_map/ppermute | solution.py:21
  5.7 0.9 select_reduce_fusion.1
  6.6 1.5 %collective-permute-done = f32[1,225,128]{2,1,0:T(8,128)S(1)} collective-permute-done((f32[1,225,128]{2,1,0:T(8,128)S(1)}, f32[1,225,128]{2,1,0:T(8,128)S(1)}, u32[]{:S(2)}, u32[]{:S(2)}) %collective-permute-start) | collective-permute-done | bytes 115232 | tf_op jit(solution)/shard_map/ppermute | solution.py:18
  8.1 0.0 copy-start.4
  8.2 4.2 %constant_dynamic-update-slice_fusion.1 = f32[34,225,128]{2,1,0:T(8,128)S(1)} fusion(f32[34,225,128]{2,1,0:T(8,128)S(1)} %constant_dynamic-update-slice_fusion.2, f32[32,225,128]{2,0,1:T(8,128)} %param.12), kind=kLoop, calls=%fused_computation.161 | loop fusion | bytes 7487488
  12.3 0.0 collective-permute-done.1
  12.4 0.0 copy-start.2
  12.4 1.9 %copy-done.2 = f32[34,225,128]{2,1,0:T(8,128)} copy-done((f32[34,225,128]{2,1,0:T(8,128)}, f32[34,225,128]{2,1,0:T(8,128)S(1)}, u32[]{:S(2)}) %copy-start.2) | copy-done | bytes 3916824
  14.3 7.5 %collective-permute-start.3 = (f32[34,1,128]{2,1,0:T(1,128)S(1)}, f32[34,1,128]{2,1,0:T(1,128)S(1)}, u32[]{:S(2)}, u32[]{:S(2)}) collective-permute-start(f32[34,1,128]{2,1,0:T(1,128)S(1)} %get-tuple-element.32), channel_id=1, source_target_pairs={{1,0},{2,1},{3,2},{4,3},{5,4},{6,5},{7,6},{8,7},{9,8},{10,9},{11,1... | collective-permute-start | bytes 52232 | tf_op jit(solution)/shard_map/ppermute | solution.py:21
  21.8 0.0 collective-permute-start.2
  21.8 0.0 copy-done.4
  21.8 0.2 convolution_select_fusion
  22.1 0.0 copy-start.5
  22.1 0.0 copy-start.6
  22.1 1.2 %collective-permute-done.3 = f32[34,1,128]{2,1,0:T(1,128)S(1)} collective-permute-done((f32[34,1,128]{2,1,0:T(1,128)S(1)}, f32[34,1,128]{2,1,0:T(1,128)S(1)}, u32[]{:S(2)}, u32[]{:S(2)}) %collective-permute-start.3) | collective-permute-done | bytes 17440 | tf_op jit(solution)/shard_map/ppermute | solution.py:21
  23.2 5.9 %collective-permute-done.2 = f32[34,1,128]{2,1,0:T(1,128)S(1)} collective-permute-done((f32[34,1,128]{2,1,0:T(1,128)S(1)}, f32[34,1,128]{2,1,0:T(1,128)S(1)}, u32[]{:S(2)}, u32[]{:S(2)}) %collective-permute-start.2) | collective-permute-done | bytes 17440 | tf_op jit(solution)/shard_map/ppermute | solution.py:18
  29.2 2.7 %maximum_multiply_fusion = f32[34,227,128]{2,1,0:T(8,128)S(1)} fusion(f32[34,1,128]{2,1,0:T(1,128)S(1)} %collective-permute-done.3, f32[34,225,128]{2,1,0:T(8,128)} %copy-done.2, f32[34,1,128]{2,1,0:T(1,128)S(1)} %collective-permute-done.2, f32[34]{0:T(128)S(1)} %constant_dynamic-update-slice_fusion.3), kind=kLoop, calls=%fused_computation.30 | loop fusion | flops 2963712 | bytes 7903368 | tf_op jit(solution)/shard_map/mul | solution.py:57
  31.9 0.0 copy-done
  31.9 0.0 copy-done.5
  31.9 0.0 copy-done.6
  31.9 0.0 copy-start.3
  31.9 5.3 %convolution_add_fusion = f32[32,225,128]{2,1,0:T(8,128)S(1)} fusion(f32[34,227,128]{2,1,0:T(8,128)S(1)} %maximum_multiply_fusion, f32[32]{0:T(128)S(1)} %copy-done.5, f32[128]{0:T(128)S(1)} %copy-done.6, f32[128,128]{1,0:T(8,128)S(1)} %copy-done), kind=kOutput, calls=%fused_computation.147 | convolution fusion | flops 1425715200 | bytes 22758400 | tf_op jit(solution)/shard_map/dot_general | solution.py:68
  37.2 0.0 copy-start.1
  37.3 0.3 collective-permute-start.5
  37.6 2.0 %collective-permute-start.4 = (f32[32,16,128]{2,1,0:T(8,128)S(1)}, f32[32,16,128]{2,1,0:T(8,128)S(1)}, u32[]{:S(2)}, u32[]{:S(2)}) collective-permute-start(f32[32,16,128]{2,1,0:T(8,128)S(1)} %get-tuple-element.33), channel_id=1, source_target_pairs={{0,1},{1,2},{2,3},{3,4},{4,5},{5,6},{6,7},{7,8},{8,9},{9,10},{10,1... | collective-permute-start | bytes 786440 | tf_op jit(solution)/shard_map/ppermute | solution.py:18
  39.6 0.0 copy-done.3
  39.6 0.2 compare_reduce_fusion
  39.8 4.1 %collective-permute-done.5 = f32[32,16,128]{2,1,0:T(8,128)S(1)} collective-permute-done((f32[32,16,128]{2,1,0:T(8,128)S(1)}, f32[32,16,128]{2,1,0:T(8,128)S(1)}, u32[]{:S(2)}, u32[]{:S(2)}) %collective-permute-start.5) | collective-permute-done | bytes 262176 | tf_op jit(solution)/shard_map/ppermute | solution.py:21
  43.9 3.7 %collective-permute-done.4 = f32[32,16,128]{2,1,0:T(8,128)S(1)} collective-permute-done((f32[32,16,128]{2,1,0:T(8,128)S(1)}, f32[32,16,128]{2,1,0:T(8,128)S(1)}, u32[]{:S(2)}, u32[]{:S(2)}) %collective-permute-start.4) | collective-permute-done | bytes 262176 | tf_op jit(solution)/shard_map/ppermute | solution.py:18
  47.6 0.0 copy-done.1
  47.6 63.8 %fusion.5 = f32[32,225,128]{2,1,0:T(8,128)S(1)} fusion(f32[32,225,128]{2,1,0:T(8,128)} %copy-done.1, f32[32,16,128]{2,1,0:T(8,128)S(1)} %collective-permute-done.5, f32[32,16,128]{2,1,0:T(8,128)S(1)} %collective-permute-done.4, f32[32]{0:T(128)S(1)} %get-tuple-element.38, f32[32]{0:T(128)S(1)} %get-tuple-element.39, f32[32]{0:T(128)S(1)} %get-tuple-element.40, ...), kind=kLoop, calls=%fused_computation.36 | loop fusion | flops 75571200 | bytes 7899296 | tf_op jit(solution)/shard_map/jit(_where)/select_n | solution.py:76
  111.4 2.5 %copy.16 = f32[32,225,128]{2,0,1:T(8,128)} copy(f32[32,225,128]{2,1,0:T(8,128)S(1)} %fusion.5) | data formatting | bytes 7372800 | tf_op jit(solution)/shard_map/jit(_where)/select_n | solution.py:76
  (10 shorter events, 0.1 us)
Async XLA Ops:
  0.0 31.9 %copy-start = (f32[128,128]{1,0:T(8,128)S(1)}, f32[128,128]{1,0:T(8,128)}, u32[]{:S(2)}) copy-start(f32[128,128]{1,0:T(8,128)} %param.15) | copy-start | bytes 196612
  1.7 6.4 %collective-permute-start = (f32[1,225,128]{2,1,0:T(8,128)S(1)}, f32[1,225,128]{2,1,0:T(8,128)S(1)}, u32[]{:S(2)}, u32[]{:S(2)}) collective-permute-start(f32[1,225,128]{2,1,0:T(8,128)S(1)} %copy.18), channel_id=1, source_target_pairs={{0,16},{16,32},{32,48},{48,64},{64,80},{80,96},{96,112},{112,128},... | collective-permute-start | bytes 345608 | tf_op jit(solution)/shard_map/ppermute | solution.py:18
  1.8 10.6 %collective-permute-start.1 = (f32[1,225,128]{2,1,0:T(8,128)S(1)}, f32[1,225,128]{2,1,0:T(8,128)S(1)}, u32[]{:S(2)}, u32[]{:S(2)}) collective-permute-start(f32[1,225,128]{2,1,0:T(8,128)S(1)} %copy.19), channel_id=1, source_target_pairs={{16,0},{32,16},{48,32},{64,48},{80,64},{96,80},{112,96},{128,112},... | collective-permute-start | bytes 345608 | tf_op jit(solution)/shard_map/ppermute | solution.py:21
  8.1 13.6 %copy-start.4 = (f32[16,17]{1,0:T(8,128)S(1)}, f32[16,17]{1,0:T(8,128)}, u32[]{:S(2)}) copy-start(f32[16,17]{1,0:T(8,128)} %param.19) | copy-start | bytes 3268
  12.4 1.9 %copy-start.2 = (f32[34,225,128]{2,1,0:T(8,128)}, f32[34,225,128]{2,1,0:T(8,128)S(1)}, u32[]{:S(2)}) copy-start(f32[34,225,128]{2,1,0:T(8,128)S(1)} %constant_dynamic-update-slice_fusion) | copy-start | bytes 11750404
  14.3 8.9 %collective-permute-start.3 = (f32[34,1,128]{2,1,0:T(1,128)S(1)}, f32[34,1,128]{2,1,0:T(1,128)S(1)}, u32[]{:S(2)}, u32[]{:S(2)}) collective-permute-start(f32[34,1,128]{2,1,0:T(1,128)S(1)} %get-tuple-element.32), channel_id=1, source_target_pairs={{1,0},{2,1},{3,2},{4,3},{5,4},{6,5},{7,6},{8,7},{9,8},{10,9},{11,1... | collective-permute-start | bytes 52232 | tf_op jit(solution)/shard_map/ppermute | solution.py:21
  21.8 7.4 %collective-permute-start.2 = (f32[34,1,128]{2,1,0:T(1,128)S(1)}, f32[34,1,128]{2,1,0:T(1,128)S(1)}, u32[]{:S(2)}, u32[]{:S(2)}) collective-permute-start(f32[34,1,128]{2,1,0:T(1,128)S(1)} %get-tuple-element.31), channel_id=1, source_target_pairs={{0,1},{1,2},{2,3},{3,4},{4,5},{5,6},{6,7},{7,8},{8,9},{9,10},{10,1... | collective-permute-start | bytes 52232 | tf_op jit(solution)/shard_map/ppermute | solution.py:18
  22.1 9.8 %copy-start.5 = (f32[32]{0:T(128)S(1)}, f32[32]{0:T(128)}, u32[]{:S(2)}) copy-start(f32[32]{0:T(128)} %param.13) | copy-start | bytes 388
  22.1 9.8 %copy-start.6 = (f32[128]{0:T(128)S(1)}, f32[128]{0:T(128)}, u32[]{:S(2)}) copy-start(f32[128]{0:T(128)} %param.14) | copy-start | bytes 1540
  31.9 7.7 %copy-start.3 = (s32[192]{0:T(256)S(1)}, s32[192]{0:T(256)}, u32[]{:S(2)}) copy-start(s32[192]{0:T(256)} %param.16) | copy-start | bytes 2308
  37.2 10.4 %copy-start.1 = (f32[32,225,128]{2,1,0:T(8,128)}, f32[32,225,128]{2,1,0:T(8,128)S(1)}, u32[]{:S(2)}) copy-start(f32[32,225,128]{2,1,0:T(8,128)S(1)} %convolution_add_fusion) | copy-start | bytes 11059204
  37.3 6.6 %collective-permute-start.5 = (f32[32,16,128]{2,1,0:T(8,128)S(1)}, f32[32,16,128]{2,1,0:T(8,128)S(1)}, u32[]{:S(2)}, u32[]{:S(2)}) collective-permute-start(f32[32,16,128]{2,1,0:T(8,128)S(1)} %get-tuple-element.34), channel_id=1, source_target_pairs={{1,0},{2,1},{3,2},{4,3},{5,4},{6,5},{7,6},{8,7},{9,8},{10,9},{11,1... | collective-permute-start | bytes 786440 | tf_op jit(solution)/shard_map/ppermute | solution.py:21
  37.6 10.1 %collective-permute-start.4 = (f32[32,16,128]{2,1,0:T(8,128)S(1)}, f32[32,16,128]{2,1,0:T(8,128)S(1)}, u32[]{:S(2)}, u32[]{:S(2)}) collective-permute-start(f32[32,16,128]{2,1,0:T(8,128)S(1)} %get-tuple-element.33), channel_id=1, source_target_pairs={{0,1},{1,2},{2,3},{3,4},{4,5},{5,6},{6,7},{7,8},{8,9},{9,10},{10,1... | collective-permute-start | bytes 786440 | tf_op jit(solution)/shard_map/ppermute | solution.py:18
where the time goes:
time: 114 us
  other arithmetic  67.6 us (59%)
  waiting for transfers between devices  16.5 us (14%)
  starting transfers between devices  13.8 us (12%)
  local copies, waits for them, and re-layouts  10.4 us (9%)
  matrix products  5.55 us (5%)
    select_n x1, other arithmetic, local(): filtered = jnp.where(listed[:, None, None], smooth, coupled_wide)  63.8 us
    ppermute x3, starting transfers between devices, extended_2(): lax.ppermute(lax.slice_in_dim(block, 0, width, axis=dim), axis, backward)  11.7 us
    ppermute x3, waiting for transfers between devices, extended_2(): lax.ppermute(lax.slice_in_dim(block, block.shape[dim] - width, None, axis...  11.1 us
    unnamed x18, local copies, waits for them, and re-layouts  6.13 us
    dot_general x1, matrix products, local(): jnp.dot(flat, coupling, precision=lax.Precision.HIGHEST, preferred_elemen...  5.34 us
    ppermute x3, waiting for transfers between devices, extended_2(): lax.ppermute(lax.slice_in_dim(block, 0, width, axis=dim), axis, backward)  5.31 us
    mul x1, other arithmetic, local(): padded = padded * keep[:, None, None]  2.7 us
    select_n x1, local copies, waits for them, and re-layouts, local(): filtered = jnp.where(listed[:, None, None], smooth, coupled_wide)  2.51 us
  transfers between devices with their start and end apart: 6, of which 5 were waited for; matrix products, arithmetic and copies ran while one was open for 5% of the time, Pallas kernels for 0%

commit v1 on v0

v1 whole, which is shorter than its diff:
```python
import jax
import jax.numpy as jnp
from jax import lax
from jax.experimental import pallas as pl
from jax.experimental.pallas import tpu as pltpu
from jax.sharding import PartitionSpec as P

MAXB = 16
HALO = MAXB + 1
MERIDIONAL = 0.1
ROWS = 32
COLS = 225
CH = 128
TILES = ROWS // 8
CHUNK = 32
BLOCK = 8
MESH = pl.DeviceIdType.MESH
F32 = jnp.float32
BF16 = jnp.bfloat16


def chunks(total, size):
    return [min(i * size, total - size) for i in range((total + size - 1) // size)]


def kernel(
    st, zc, df, cp, fr, bw, ti, ct, out,
    S, C, W, A, C0, R, zc_v, df_v, cp_v, fr_v, bw_v, ti_v, ct_v, ss, rs, ls,
):
    la = lax.axis_index("lat")
    lo = lax.axis_index("lon")
    east = lax.rem(lo + 1, 16)
    west = lax.rem(lo + 15, 16)

    def is_polar(pos):
        return (pos < 4) | (pos >= 12)

    polar = is_polar(la)
    has_up = la < 15
    has_down = la > 0
    corner_up = has_up & (polar | is_polar(la + 1))
    corner_down = has_down & (polar | is_polar(la - 1))

    barrier = pltpu.get_barrier_semaphore()

    def greet(*who):
        for device in who:
            pl.semaphore_signal(barrier, inc=1, device_id=device, device_id_type=MESH)

    greet((la, east), (la, west))
    pl.when(has_up)(lambda: greet((la + 1, lo)))
    pl.when(has_down)(lambda: greet((la - 1, lo)))
    pl.when(corner_up)(lambda: greet((la + 1, east), (la + 1, west)))
    pl.when(corner_down)(lambda: greet((la - 1, east), (la - 1, west)))

    small = [(zc, zc_v), (df, df_v), (cp, cp_v), (fr, fr_v), (bw, bw_v), (ti, ti_v), (ct, ct_v)]
    loads = [pltpu.make_async_copy(src, dst, ls.at[i]) for i, (src, dst) in enumerate(small)]
    body = pltpu.make_async_copy(st, S.at[HALO : HALO + COLS, 8 : 8 + ROWS], ls.at[7])
    body.start()
    for load in loads:
        load.start()

    count = (
        2
        + jnp.where(has_up, 1, 0)
        + jnp.where(has_down, 1, 0)
        + jnp.where(corner_up, 2, 0)
        + jnp.where(corner_down, 2, 0)
    )
    pl.semaphore_wait(barrier, count)

    def send(src, dst, i, device):
        return pltpu.make_async_remote_copy(
            src_ref=src, dst_ref=dst, send_sem=ss.at[i], recv_sem=rs.at[i],
            device_id=device, device_id_type=MESH,
        )

    last = COLS - HALO
    high = HALO + COLS
    wide = []
    for t in range(TILES):
        here, there = slice(8 * t, 8 * t + 8), slice(8 * t + 8, 8 * t + 16)
        wide.append(
            (
                send(st.at[last:COLS, here], S.at[0:HALO, there], 2 * t, (la, east)),
                send(st.at[0:HALO, here], S.at[high : high + HALO, there], 2 * t + 1, (la, west)),
            )
        )
    thin = (
        send(st.at[COLS - 1 : COLS], S.at[HALO - 1 : HALO, 8 : 8 + ROWS], 0, (la, east)),
        send(st.at[0:1], S.at[high : high + 1, 8 : 8 + ROWS], 1, (la, west)),
    )
    up = send(st.at[:, 31:32], S.at[HALO:high, 7:8], 8, (la + 1, lo))
    down = send(st.at[:, 0:1], S.at[HALO:high, 40:41], 9, (la - 1, lo))
    up_east = send(st.at[last:COLS, 31:32], S.at[0:HALO, 7:8], 10, (la + 1, east))
    up_west = send(st.at[0:HALO, 31:32], S.at[high : high + HALO, 7:8], 11, (la + 1, west))
    down_east = send(st.at[last:COLS, 0:1], S.at[0:HALO, 40:41], 12, (la - 1, east))
    down_west = send(st.at[0:HALO, 0:1], S.at[high : high + HALO, 40:41], 13, (la - 1, west))

    def start(*copies):
        for copy in copies:
            copy.start()

    def wait_send(*copies):
        for copy in copies:
            copy.wait_send()

    def wait_recv(*copies):
        for copy in copies:
            copy.wait_recv()

    pl.when(polar)(lambda: start(*[copy for pair in wide for copy in pair]))
    pl.when(jnp.logical_not(polar))(lambda: start(*thin))
    pl.when(has_up)(lambda: start(up))
    pl.when(has_down)(lambda: start(down))
    to_up = has_up & is_polar(la + 1)
    to_down = has_down & is_polar(la - 1)
    pl.when(to_up)(lambda: start(up_east, up_west))
    pl.when(to_down)(lambda: start(down_east, down_west))

    def clear(row):
        S[:, row : row + 1, :] = jnp.zeros((S.shape[0], 1, CH), F32)

    pl.when(jnp.logical_not(has_down))(lambda: clear(7))
    pl.when(jnp.logical_not(has_up))(lambda: clear(40))

    for load in loads:
        load.wait()

    def iota(shape, dim):
        return lax.broadcasted_iota(jnp.int32, shape, dim)

    def column(values, offset):
        width = values.shape[1]
        pick = iota((ROWS, width), 1) == iota((ROWS, width), 0) + offset
        return jnp.sum(jnp.where(pick, values.astype(F32), 0.0), axis=1, keepdims=True)

    zonal = column(zc_v[...], 0)
    spread = df_v[...]
    A[...] = zonal * spread
    C0[...] = 1.0 - 2.0 * (zonal + MERIDIONAL) * spread
    fine = cp_v[...]
    coarse = fine.astype(BF16)
    rest = (fine - coarse.astype(F32)).astype(BF16)
    both = jnp.concatenate([coarse, rest], axis=1)
    R[...] = jnp.concatenate([both, both], axis=0)

    @pl.when(polar)
    def _():
        first = la * ROWS
        tables = column(ti_v[...], first)
        widths = column(bw_v[...], first)
        same = fr_v[...] == iota((ROWS, fr_v.shape[1]), 0) + first
        listed = jnp.sum(jnp.where(same, 1.0, 0.0), axis=1, keepdims=True) > 0.5
        taps = ct_v.shape[1]
        picked = jnp.zeros((ROWS, taps), F32)
        for table in range(ct_v.shape[0]):
            picked = jnp.where(tables == float(table), ct_v[table : table + 1, :], picked)
        reach = iota((ROWS, taps), 1)
        picked = jnp.where(reach.astype(F32) <= widths, picked, 0.0)
        picked = jnp.where(listed, picked, jnp.where(reach == 0, 1.0, 0.0))
        for k in range(taps):
            W[k] = jnp.broadcast_to(picked[:, k : k + 1], (ROWS, CH)).reshape(TILES, 8, CH)

    def couple(t, q0, size):
        low = 8 + 8 * t
        centre = S[pl.ds(q0 + 1, size), low : low + 8, :]
        sides = S[pl.ds(q0 + 2, size), low : low + 8, :] + S[pl.ds(q0, size), low : low + 8, :]
        poles = (
            S[pl.ds(q0 + 1, size), low + 1 : low + 9, :]
            + S[pl.ds(q0 + 1, size), low - 1 : low + 7, :]
        )
        rows = slice(8 * t, 8 * t + 8)
        stepped = (
            C0[rows][None] * centre
            + A[rows][None] * sides
            + (MERIDIONAL * df_v[...])[None] * poles
        )
        flat = stepped.reshape(size * 8, CH)
        big = flat.astype(BF16)
        small = (flat - big.astype(F32)).astype(BF16)
        wide = jnp.dot(
            jnp.concatenate([big, small], axis=1), R[...], preferred_element_type=F32
        )
        return (flat + (wide[:, :CH] + wide[:, CH:])).reshape(size, 8, CH)

    def smooth(t, i0):
        window = [C[t, i0 + m] for m in range(BLOCK + 2 * MAXB)]
        total = [W[0, t] * window[b + MAXB] for b in range(BLOCK)]
        for k in range(1, MAXB + 1):
            weight = W[k, t]
            for b in range(BLOCK):
                total[b] = total[b] + weight * (window[b + MAXB - k] + window[b + MAXB + k])
        for b in range(BLOCK):
            out[i0 + b, pl.ds(pl.multiple_of(8 * t, 8), 8), :] = total[b]

    def inner(t):
        n = COLS - 2
        steps = (n + CHUNK - 1) // CHUNK

        @pl.loop(0, steps)
        def _(j):
            q0 = HALO + jnp.minimum(j * CHUNK, n - CHUNK)
            C[t, pl.ds(q0, CHUNK)] = couple(t, q0, CHUNK)

        m = COLS - 2 * HALO
        steps = (m + BLOCK - 1) // BLOCK

        @pl.loop(0, steps)
        def _(j):
            smooth(t, HALO + jnp.minimum(j * BLOCK, m - BLOCK))

    def edges(t):
        C[t, 0:HALO] = couple(t, 0, HALO)
        C[t, COLS + MAXB - 1 : COLS + 2 * MAXB] = couple(t, COLS + MAXB - 1, HALO)

        @pl.loop(0, 6)
        def _(j):
            left = jnp.minimum(j * BLOCK, HALO - BLOCK)
            right = COLS - HALO + jnp.minimum((j - 3) * BLOCK, HALO - BLOCK)
            smooth(t, jnp.where(j < 3, left, right))

    def plain(t):
        steps = (COLS + CHUNK - 1) // CHUNK

        @pl.loop(0, steps)
        def _(j):
            i0 = jnp.minimum(j * CHUNK, COLS - CHUNK)
            out[pl.ds(i0, CHUNK), 8 * t : 8 * t + 8, :] = couple(t, i0 + MAXB, CHUNK)

    body.wait()

    @pl.when(polar)
    def _():
        inner(1)
        inner(2)

    pl.when(has_down)(lambda: wait_recv(up))
    pl.when(has_up)(lambda: wait_recv(down))

    @pl.when(polar)
    def _():
        inner(0)
        inner(3)
        pl.when(has_down)(lambda: wait_recv(up_east, up_west))
        pl.when(has_up)(lambda: wait_recv(down_east, down_west))
        wait_recv(*wide[0])
        for t in range(TILES):
            if t + 1 < TILES:
                wait_recv(*wide[t + 1])
            edges(t)

    @pl.when(jnp.logical_not(polar))
    def _():
        wait_recv(*thin)
        for t in range(TILES):
            plain(t)

    pl.when(polar)(lambda: wait_send(*[copy for pair in wide for copy in pair]))
    pl.when(jnp.logical_not(polar))(lambda: wait_send(*thin))
    pl.when(has_up)(lambda: wait_send(up))
    pl.when(has_down)(lambda: wait_send(down))
    pl.when(to_up)(lambda: wait_send(up_east, up_west))
    pl.when(to_down)(lambda: wait_send(down_east, down_west))


def local(
    state, zonal_coef, diffusivity, coupling, filter_rows, band_width, table_index, coef_table
):
    turned = jnp.transpose(state, (1, 0, 2))
    args = (
        turned, zonal_coef[None, :], diffusivity[None, :], coupling,
        filter_rows[None, :], band_width[None, :], table_index[None, :], coef_table,
    )
    updated = pl.pallas_call(
        kernel,
        out_shape=jax.ShapeDtypeStruct((COLS, ROWS, CH), F32),
        in_specs=[pl.BlockSpec(memory_space=pl.ANY)] * len(args),
        out_specs=pl.BlockSpec(memory_space=pltpu.VMEM),
        scratch_shapes=[
            pltpu.VMEM((COLS + 2 * HALO, ROWS + 16, CH), F32),
            pltpu.VMEM((TILES, COLS + 2 * MAXB, 8, CH), F32),
            pltpu.VMEM((MAXB + 1, TILES, 8, CH), F32),
            pltpu.VMEM((ROWS, CH), F32),
            pltpu.VMEM((ROWS, CH), F32),
            pltpu.VMEM((2 * CH, 2 * CH), BF16),
        ]
        + [pltpu.VMEM(a.shape, a.dtype) for a in args[1:]]
        + [
            pltpu.SemaphoreType.DMA((14,)),
            pltpu.SemaphoreType.DMA((14,)),
            pltpu.SemaphoreType.DMA((8,)),
        ],
        compiler_params=pltpu.CompilerParams(
            collective_id=0, has_side_effects=True, vmem_limit_bytes=56 * 1024 * 1024
        ),
    )(*args)
    return jnp.transpose(updated, (1, 0, 2))


def solution(mesh):
    return jax.shard_map(
        local,
        mesh=mesh,
        in_specs=(P("lat", "lon", None), P("lat"), P(), P(), P(), P(), P(), P()),
        out_specs=P("lat", "lon", None),
        check_vma=False,
    )
```

time: 114 us -> 33.4 us (0.29)
  the two profiles are of different devices: /device:TPU:2 before, /device:TPU:1 now
where the time goes in v1:
time: 33.4 us; the launch traced here: 33.3 us
  Pallas kernels  29 us (87%)
  local copies, waits for them, and re-layouts  4.26 us (13%)
    pallas_call x1, Pallas kernels, local(): pl.pallas_call(kernel, out_shape=jax.ShapeDtypeStruct((COLS, ROWS, CH), F...  29 us
    unnamed x1, local copies, waits for them, and re-layouts  4.26 us

profile of v1, /device:TPU:1, one launch (start us, length us, event | category | flops | bytes accessed | tf_op | source)
XLA Modules:
  0.0 33.3 jit_solution(10906081795718661376)
XLA Ops:
  0.0 29.0 %shard_map.82 = f32[225,32,128]{2,1,0:T(8,128)} custom-call(f32[225,32,128]{2,1,0:T(8,128)} %bitcast.8, f32[1,32]{1,0:T(1,128)} %bitcast.12, f32[1,128]{1,0:T(1,128)} %bitcast.13, f32[128,128]{1,0:T(8,128)} %cp.1, s32[1,192]{1,0:T(1,128)} %bitcast.11, s32[1,512]{1,0:T(1,128)} %bitcast.9, s32[1,512]{1,0:T(1,128)} %bitcast.10, f32[16,17]{1,0:T(8,128)} %ct.1), custom_call_target="tpu_custom_call" | custom-call | tf_op jit(solution)/shard_map/pallas_call | solution.py:275
  29.0 4.3 %copy.10 = f32[32,225,128]{2,0,1:T(8,128)} copy(f32[32,225,128]{2,0,1:T(8,128)} %bitcast.7) | data formatting | bytes 7372800

commit v2 on v1

--- a/solution.py
+++ b/solution.py
@@ -12,7 +12,8 @@
 COLS = 225
 CH = 128
 TILES = ROWS // 8
-CHUNK = 32
+CHUNK = 112
+PLAIN = 75
 BLOCK = 8
 MESH = pl.DeviceIdType.MESH
 F32 = jnp.float32
@@ -59,6 +60,128 @@
     body.start()
     for load in loads:
         load.start()
+
+    def prepare():
+        for load in loads:
+            load.wait()
+        body.wait()
+
+        def iota(shape, dim):
+            return lax.broadcasted_iota(jnp.int32, shape, dim)
+
+        def column(values, offset):
+            width = values.shape[1]
+            pick = iota((ROWS, width), 1) == iota((ROWS, width), 0) + offset
+            return jnp.sum(jnp.where(pick, values.astype(F32), 0.0), axis=1, keepdims=True)
+
+        zonal = column(zc_v[...], 0)
+        spread = df_v[...]
+        A[...] = zonal * spread
+        C0[...] = 1.0 - 2.0 * (zonal + MERIDIONAL) * spread
+        fine = cp_v[...]
+        coarse = fine.astype(BF16)
+        rest = (fine - coarse.astype(F32)).astype(BF16)
+        both = jnp.concatenate([coarse, rest], axis=1)
+        R[...] = jnp.concatenate([both, both], axis=0)
+
+        @pl.when(polar)
+        def _():
+            first = la * ROWS
+            tables = column(ti_v[...], first)
+            widths = column(bw_v[...], first)
+            same = fr_v[...] == iota((ROWS, fr_v.shape[1]), 0) + first
+            listed = jnp.sum(jnp.where(same, 1.0, 0.0), axis=1, keepdims=True) > 0.5
+            taps = ct_v.shape[1]
+            picked = jnp.zeros((ROWS, taps), F32)
+            for table in range(ct_v.shape[0]):
+                picked = jnp.where(tables == float(table), ct_v[table : table + 1, :], picked)
+            reach = iota((ROWS, taps), 1)
+            picked = jnp.where(reach.astype(F32) <= widths, picked, 0.0)
+            picked = jnp.where(listed, picked, jnp.where(reach == 0, 1.0, 0.0))
+            for k in range(taps):
+                W[k] = jnp.broadcast_to(picked[:, k : k + 1], (ROWS, CH)).reshape(TILES, 8, CH)
+
+    def stepped(t, q0, size):
+        low = 8 + 8 * t
+        centre = S[pl.ds(q0 + 1, size), low : low + 8, :]
+        sides = S[pl.ds(q0 + 2, size), low : low + 8, :] + S[pl.ds(q0, size), low : low + 8, :]
+        poles = (
+            S[pl.ds(q0 + 1, size), low + 1 : low + 9, :]
+            + S[pl.ds(q0 + 1, size), low - 1 : low + 7, :]
+        )
+        rows = slice(8 * t, 8 * t + 8)
+        value = (
+            C0[rows][None] * centre
+            + A[rows][None] * sides
+            + (MERIDIONAL * df_v[...])[None] * poles
+        )
+        return value.reshape(size * 8, CH)
+
+    def couple(*parts):
+        flat = [stepped(*part) for part in parts]
+        flat = flat[0] if len(flat) == 1 else jnp.concatenate(flat, axis=0)
+        big = flat.astype(BF16)
+        small = (flat - big.astype(F32)).astype(BF16)
+        wide = jnp.dot(
+            jnp.concatenate([big, small], axis=1), R[...], preferred_element_type=F32
+        )
+        flat = flat + (wide[:, :CH] + wide[:, CH:])
+        return flat.reshape(flat.shape[0] // 8, 8, CH)
+
+    def smooth(t, i0, size):
+        window = [C[t, i0 + m] for m in range(size + 2 * MAXB)]
+        total = [W[0, t] * window[b + MAXB] for b in range(size)]
+        for k in range(1, MAXB + 1):
+            weight = W[k, t]
+            for b in range(size):
+                total[b] = total[b] + weight * (window[b + MAXB - k] + window[b + MAXB + k])
+        for b in range(size):
+            out[i0 + b, pl.ds(pl.multiple_of(8 * t, 8), 8), :] = total[b]
+
+    def inner(t):
+        n = COLS - 2
+        steps = (n + CHUNK - 1) // CHUNK
+
+        @pl.loop(0, steps)
+        def _(j):
+            q0 = HALO + jnp.minimum(j * CHUNK, n - CHUNK)
+            C[t, pl.ds(q0, CHUNK)] = couple((t, q0, CHUNK))
+
+        m = COLS - 2 * HALO
+        steps = (m + BLOCK - 1) // BLOCK
+
+        @pl.loop(0, steps)
+        def _(j):
+            smooth(t, HALO + jnp.minimum(j * BLOCK, m - BLOCK), BLOCK)
+
+    def edges(*tiles):
+        far = COLS + MAXB - 1
+        parts = [(t, q0, HALO) for t in tiles for q0 in (0, far)]
+        value = couple(*parts)
+        for i, (t, q0, size) in enumerate(parts):
+            C[t, q0 : q0 + size] = value[i * size : i * size + size]
+        for t in tiles:
+
+            @pl.loop(0, 2)
+            def _(j):
+                smooth(t, j * (COLS - HALO), HALO)
+
+    def plain(t):
+        @pl.loop(0, COLS // PLAIN)
+        def _(j):
+            i0 = j * PLAIN
+            out[pl.ds(i0, PLAIN), 8 * t : 8 * t + 8, :] = couple((t, i0 + MAXB, PLAIN))
+
+    def ahead():
+        prepare()
+
+        @pl.when(polar)
+        def _():
+            inner(1)
+            inner(2)
+
+    early = lax.rem(lo, 8) == 0
+    pl.when(early)(ahead)
 
     count = (
         2
@@ -124,116 +247,7 @@
     pl.when(jnp.logical_not(has_down))(lambda: clear(7))
     pl.when(jnp.logical_not(has_up))(lambda: clear(40))
 
-    for load in loads:
-        load.wait()
-
-    def iota(shape, dim):
-        return lax.broadcasted_iota(jnp.int32, shape, dim)
-
-    def column(values, offset):
-        width = values.shape[1]
-        pick = iota((ROWS, width), 1) == iota((ROWS, width), 0) + offset
-        return jnp.sum(jnp.where(pick, values.astype(F32), 0.0), axis=1, keepdims=True)
-
-    zonal = column(zc_v[...], 0)
-    spread = df_v[...]
-    A[...] = zonal * spread
-    C0[...] = 1.0 - 2.0 * (zonal + MERIDIONAL) * spread
-    fine = cp_v[...]
-    coarse = fine.astype(BF16)
-    rest = (fine - coarse.astype(F32)).astype(BF16)
-    both = jnp.concatenate([coarse, rest], axis=1)
-    R[...] = jnp.concatenate([both, both], axis=0)
-
-    @pl.when(polar)
-    def _():
-        first = la * ROWS
-        tables = column(ti_v[...], first)
-        widths = column(bw_v[...], first)
-        same = fr_v[...] == iota((ROWS, fr_v.shape[1]), 0) + first
-        listed = jnp.sum(jnp.where(same, 1.0, 0.0), axis=1, keepdims=True) > 0.5
-        taps = ct_v.shape[1]
-        picked = jnp.zeros((ROWS, taps), F32)
-        for table in range(ct_v.shape[0]):
-            picked = jnp.where(tables == float(table), ct_v[table : table + 1, :], picked)
-        reach = iota((ROWS, taps), 1)
-        picked = jnp.where(reach.astype(F32) <= widths, picked, 0.0)
-        picked = jnp.where(listed, picked, jnp.where(reach == 0, 1.0, 0.0))
-        for k in range(taps):
-            W[k] = jnp.broadcast_to(picked[:, k : k + 1], (ROWS, CH)).reshape(TILES, 8, CH)
-
-    def couple(t, q0, size):
-        low = 8 + 8 * t
-        centre = S[pl.ds(q0 + 1, size), low : low + 8, :]
-        sides = S[pl.ds(q0 + 2, size), low : low + 8, :] + S[pl.ds(q0, size), low : low + 8, :]
-        poles = (
-            S[pl.ds(q0 + 1, size), low + 1 : low + 9, :]
-            + S[pl.ds(q0 + 1, size), low - 1 : low + 7, :]
-        )
-        rows = slice(8 * t, 8 * t + 8)
-        stepped = (
-            C0[rows][None] * centre
-            + A[rows][None] * sides
-            + (MERIDIONAL * df_v[...])[None] * poles
-        )
-        flat = stepped.reshape(size * 8, CH)
-        big = flat.astype(BF16)
-        small = (flat - big.astype(F32)).astype(BF16)
-        wide = jnp.dot(
-            jnp.concatenate([big, small], axis=1), R[...], preferred_element_type=F32
-        )
-        return (flat + (wide[:, :CH] + wide[:, CH:])).reshape(size, 8, CH)
-
-    def smooth(t, i0):
-        window = [C[t, i0 + m] for m in range(BLOCK + 2 * MAXB)]
-        total = [W[0, t] * window[b + MAXB] for b in range(BLOCK)]
-        for k in range(1, MAXB + 1):
-            weight = W[k, t]
-            for b in range(BLOCK):
-                total[b] = total[b] + weight * (window[b + MAXB - k] + window[b + MAXB + k])
-        for b in range(BLOCK):
-            out[i0 + b, pl.ds(pl.multiple_of(8 * t, 8), 8), :] = total[b]
-
-    def inner(t):
-        n = COLS - 2
-        steps = (n + CHUNK - 1) // CHUNK
-
-        @pl.loop(0, steps)
-        def _(j):
-            q0 = HALO + jnp.minimum(j * CHUNK, n - CHUNK)
-            C[t, pl.ds(q0, CHUNK)] = couple(t, q0, CHUNK)
-
-        m = COLS - 2 * HALO
-        steps = (m + BLOCK - 1) // BLOCK
-
-        @pl.loop(0, steps)
-        def _(j):
-            smooth(t, HALO + jnp.minimum(j * BLOCK, m - BLOCK))
-
-    def edges(t):
-        C[t, 0:HALO] = couple(t, 0, HALO)
-        C[t, COLS + MAXB - 1 : COLS + 2 * MAXB] = couple(t, COLS + MAXB - 1, HALO)
-
-        @pl.loop(0, 6)
-        def _(j):
-            left = jnp.minimum(j * BLOCK, HALO - BLOCK)
-            right = COLS - HALO + jnp.minimum((j - 3) * BLOCK, HALO - BLOCK)
-            smooth(t, jnp.where(j < 3, left, right))
-
-    def plain(t):
-        steps = (COLS + CHUNK - 1) // CHUNK
-
-        @pl.loop(0, steps)
-        def _(j):
-            i0 = jnp.minimum(j * CHUNK, COLS - CHUNK)
-            out[pl.ds(i0, CHUNK), 8 * t : 8 * t + 8, :] = couple(t, i0 + MAXB, CHUNK)
-
-    body.wait()
-
-    @pl.when(polar)
-    def _():
-        inner(1)
-        inner(2)
+    pl.when(jnp.logical_not(early))(ahead)
 
     pl.when(has_down)(lambda: wait_recv(up))
     pl.when(has_up)(lambda: wait_recv(down))
@@ -245,10 +259,12 @@
         pl.when(has_down)(lambda: wait_recv(up_east, up_west))
         pl.when(has_up)(lambda: wait_recv(down_east, down_west))
         wait_recv(*wide[0])
-        for t in range(TILES):
-            if t + 1 < TILES:
-                wait_recv(*wide[t + 1])
-            edges(t)
+        wait_recv(*wide[1])
+        edges(0)
+        wait_recv(*wide[2])
+        edges(1)
+        wait_recv(*wide[3])
+        edges(2, 3)
 
     @pl.when(jnp.logical_not(polar))
     def _():
@@ -274,7 +290,7 @@
     )
     updated = pl.pallas_call(
         kernel,
-        out_shape=jax.ShapeDtypeStruct((COLS, ROWS, CH), F32),
+        out_shape=pltpu.VMEM((COLS, ROWS, CH), F32),
         in_specs=[pl.BlockSpec(memory_space=pl.ANY)] * len(args),
         out_specs=pl.BlockSpec(memory_space=pltpu.VMEM),
         scratch_shapes=[

time: 33.4 us -> 23 us (0.69)
  Pallas kernels: 29 us -> 21.1 us
  local copies, waits for them, and re-layouts: 4.26 us -> 1.84 us
    pallas_call x1, Pallas kernels: 29 us -> 21.1 us  [local(): pl.pallas_call(kernel, out_shape=pltpu.VMEM((COLS, ROWS, CH), F32), in_sp...]
    unnamed x1, local copies, waits for them, and re-layouts: 4.26 us -> 1.84 us
where the time goes in v2:
time: 23 us; the launch traced here: 22.9 us
  Pallas kernels  21.1 us (92%)
  local copies, waits for them, and re-layouts  1.84 us (8%)
    pallas_call x1, Pallas kernels, local(): pl.pallas_call(kernel, out_shape=pltpu.VMEM((COLS, ROWS, CH), F32), in_sp...  21.1 us
    unnamed x1, local copies, waits for them, and re-layouts  1.84 us

profile of v2, /device:TPU:1, one launch (start us, length us, event | category | flops | bytes accessed | tf_op | source)
XLA Modules:
  0.0 22.9 jit_solution(5782018538388972164)
XLA Ops:
  0.0 21.1 %shard_map.82 = f32[225,32,128]{2,1,0:T(8,128)S(1)} custom-call(f32[225,32,128]{2,1,0:T(8,128)} %bitcast.8, f32[1,32]{1,0:T(1,128)} %bitcast.12, f32[1,128]{1,0:T(1,128)} %bitcast.13, f32[128,128]{1,0:T(8,128)} %cp.1, s32[1,192]{1,0:T(1,128)} %bitcast.11, s32[1,512]{1,0:T(1,128)} %bitcast.9, s32[1,512]{1,0:T(1,128)} %bitcast.10, f32[16,17]{1,0:T(8,128)} %ct.1), custom_call_target="tpu_custom_call" | custom-call | tf_op jit(solution)/shard_map/pallas_call | solution.py:291
  21.1 1.8 %copy.10 = f32[32,225,128]{2,0,1:T(8,128)} copy(f32[32,225,128]{2,0,1:T(8,128)S(1)} %bitcast.7) | data formatting | bytes 7372800

commit v3 on v2

--- a/solution.py
+++ b/solution.py
@@ -27,6 +27,7 @@
 def kernel(
     st, zc, df, cp, fr, bw, ti, ct, out,
     S, C, W, A, C0, R, zc_v, df_v, cp_v, fr_v, bw_v, ti_v, ct_v, ss, rs, ls,
+    from_east, from_west,
 ):
     la = lax.axis_index("lat")
     lo = lax.axis_index("lon")
@@ -48,11 +49,24 @@
         for device in who:
             pl.semaphore_signal(barrier, inc=1, device_id=device, device_id_type=MESH)
 
-    greet((la, east), (la, west))
+    first = lax.rem(lo, 8) == 0
+    final = lax.rem(lo, 8) == 7
+    middle = jnp.logical_not(first)
+    going = jnp.logical_not(final)
+    neighbours = 1 + jnp.where(corner_up, 1, 0) + jnp.where(corner_down, 1, 0)
+
+    def tell(semaphore, side):
+        def one(device):
+            pl.semaphore_signal(semaphore, inc=1, device_id=device, device_id_type=MESH)
+
+        one((la, side))
+        pl.when(corner_up)(lambda: one((la + 1, side)))
+        pl.when(corner_down)(lambda: one((la - 1, side)))
+
+    pl.when(going)(lambda: tell(barrier, east))
+    pl.when(first)(lambda: tell(barrier, west))
     pl.when(has_up)(lambda: greet((la + 1, lo)))
     pl.when(has_down)(lambda: greet((la - 1, lo)))
-    pl.when(corner_up)(lambda: greet((la + 1, east), (la + 1, west)))
-    pl.when(corner_down)(lambda: greet((la - 1, east), (la - 1, west)))
 
     small = [(zc, zc_v), (df, df_v), (cp, cp_v), (fr, fr_v), (bw, bw_v), (ti, ti_v), (ct, ct_v)]
     loads = [pltpu.make_async_copy(src, dst, ls.at[i]) for i, (src, dst) in enumerate(small)]
@@ -180,15 +194,11 @@
             inner(1)
             inner(2)
 
-    early = lax.rem(lo, 8) == 0
-    pl.when(early)(ahead)
-
     count = (
-        2
-        + jnp.where(has_up, 1, 0)
+        jnp.where(has_up, 1, 0)
         + jnp.where(has_down, 1, 0)
-        + jnp.where(corner_up, 2, 0)
-        + jnp.where(corner_down, 2, 0)
+        + jnp.where(first, 0, neighbours)
+        + jnp.where(final, neighbours, 0)
     )
     pl.semaphore_wait(barrier, count)
 
@@ -232,14 +242,38 @@
         for copy in copies:
             copy.wait_recv()
 
-    pl.when(polar)(lambda: start(*[copy for pair in wide for copy in pair]))
-    pl.when(jnp.logical_not(polar))(lambda: start(*thin))
+    to_up = has_up & is_polar(la + 1)
+    to_down = has_down & is_polar(la - 1)
+
+    def start_east():
+        pl.when(polar)(lambda: start(*[pair[0] for pair in wide]))
+        pl.when(jnp.logical_not(polar))(lambda: start(thin[0]))
+        pl.when(to_up)(lambda: start(up_east))
+        pl.when(to_down)(lambda: start(down_east))
+
+    def start_west():
+        pl.when(polar)(lambda: start(*[pair[1] for pair in wide]))
+        pl.when(jnp.logical_not(polar))(lambda: start(thin[1]))
+        pl.when(to_up)(lambda: start(up_west))
+        pl.when(to_down)(lambda: start(down_west))
+
+    @pl.when(final)
+    def _():
+        start_east()
+        tell(from_west, east)
+
+    @pl.when(middle)
+    def _():
+        tell(from_east, west)
+        start_west()
+
     pl.when(has_up)(lambda: start(up))
     pl.when(has_down)(lambda: start(down))
-    to_up = has_up & is_polar(la + 1)
-    to_down = has_down & is_polar(la - 1)
-    pl.when(to_up)(lambda: start(up_east, up_west))
-    pl.when(to_down)(lambda: start(down_east, down_west))
+
+    @pl.when(going)
+    def _():
+        pl.semaphore_wait(from_east, neighbours)
+        start_east()
 
     def clear(row):
         S[:, row : row + 1, :] = jnp.zeros((S.shape[0], 1, CH), F32)
@@ -247,7 +281,12 @@
     pl.when(jnp.logical_not(has_down))(lambda: clear(7))
     pl.when(jnp.logical_not(has_up))(lambda: clear(40))
 
-    pl.when(jnp.logical_not(early))(ahead)
+    ahead()
+
+    @pl.when(first)
+    def _():
+        pl.semaphore_wait(from_west, neighbours)
+        start_west()
 
     pl.when(has_down)(lambda: wait_recv(up))
     pl.when(has_up)(lambda: wait_recv(down))
@@ -306,6 +345,8 @@
             pltpu.SemaphoreType.DMA((14,)),
             pltpu.SemaphoreType.DMA((14,)),
             pltpu.SemaphoreType.DMA((8,)),
+            pltpu.SemaphoreType.REGULAR,
+            pltpu.SemaphoreType.REGULAR,
         ],
         compiler_params=pltpu.CompilerParams(
             collective_id=0, has_side_effects=True, vmem_limit_bytes=56 * 1024 * 1024

time: 23 us -> 23 us (level)
  no operation moved by 1% of the time
where the time goes in v3:
time: 23 us; the launch traced here: 22.9 us
  Pallas kernels  21.1 us (92%)
  local copies, waits for them, and re-layouts  1.84 us (8%)
    pallas_call x1, Pallas kernels, local(): pl.pallas_call(kernel, out_shape=pltpu.VMEM((COLS, ROWS, CH), F32), in_sp...  21.1 us
    unnamed x1, local copies, waits for them, and re-layouts  1.84 us

profile of v3, /device:TPU:1, one launch (start us, length us, event | category | flops | bytes accessed | tf_op | source)
XLA Modules:
  0.0 22.9 jit_solution(2844858324166327936)
XLA Ops:
  0.0 21.1 %shard_map.82 = f32[225,32,128]{2,1,0:T(8,128)S(1)} custom-call(f32[225,32,128]{2,1,0:T(8,128)} %bitcast.8, f32[1,32]{1,0:T(1,128)} %bitcast.12, f32[1,128]{1,0:T(1,128)} %bitcast.13, f32[128,128]{1,0:T(8,128)} %cp.1, s32[1,192]{1,0:T(1,128)} %bitcast.11, s32[1,512]{1,0:T(1,128)} %bitcast.9, s32[1,512]{1,0:T(1,128)} %bitcast.10, f32[16,17]{1,0:T(8,128)} %ct.1), custom_call_target="tpu_custom_call" | custom-call | tf_op jit(solution)/shard_map/pallas_call | solution.py:330
  21.1 1.8 %copy.10 = f32[32,225,128]{2,0,1:T(8,128)} copy(f32[32,225,128]{2,0,1:T(8,128)S(1)} %bitcast.7) | data formatting | bytes 7372800

commit v4 on v3

--- a/solution.py
+++ b/solution.py
@@ -71,9 +71,13 @@
     small = [(zc, zc_v), (df, df_v), (cp, cp_v), (fr, fr_v), (bw, bw_v), (ti, ti_v), (ct, ct_v)]
     loads = [pltpu.make_async_copy(src, dst, ls.at[i]) for i, (src, dst) in enumerate(small)]
     body = pltpu.make_async_copy(st, S.at[HALO : HALO + COLS, 8 : 8 + ROWS], ls.at[7])
-    body.start()
-    for load in loads:
-        load.start()
+
+    def fetch():
+        body.start()
+        for load in loads:
+            load.start()
+
+    pl.when(first)(fetch)
 
     def prepare():
         for load in loads:
@@ -269,6 +273,7 @@
 
     pl.when(has_up)(lambda: start(up))
     pl.when(has_down)(lambda: start(down))
+    pl.when(middle)(fetch)
 
     @pl.when(going)
     def _():

time: 23 us -> 23 us (level)
  no operation moved by 1% of the time
where the time goes in v4:
time: 23 us; the launch traced here: 22.9 us
  Pallas kernels  21.1 us (92%)
  local copies, waits for them, and re-layouts  1.84 us (8%)
    pallas_call x1, Pallas kernels, local(): pl.pallas_call(kernel, out_shape=pltpu.VMEM((COLS, ROWS, CH), F32), in_sp...  21.1 us
    unnamed x1, local copies, waits for them, and re-layouts  1.84 us

profile of v4, /device:TPU:1, one launch (start us, length us, event | category | flops | bytes accessed | tf_op | source)
XLA Modules:
  0.0 22.9 jit_solution(5068580651859474112)
XLA Ops:
  0.0 21.1 %shard_map.82 = f32[225,32,128]{2,1,0:T(8,128)S(1)} custom-call(f32[225,32,128]{2,1,0:T(8,128)} %bitcast.8, f32[1,32]{1,0:T(1,128)} %bitcast.12, f32[1,128]{1,0:T(1,128)} %bitcast.13, f32[128,128]{1,0:T(8,128)} %cp.1, s32[1,192]{1,0:T(1,128)} %bitcast.11, s32[1,512]{1,0:T(1,128)} %bitcast.9, s32[1,512]{1,0:T(1,128)} %bitcast.10, f32[16,17]{1,0:T(8,128)} %ct.1), custom_call_target="tpu_custom_call" | custom-call | tf_op jit(solution)/shard_map/pallas_call | solution.py:335
  21.1 1.8 %copy.10 = f32[32,225,128]{2,0,1:T(8,128)} copy(f32[32,225,128]{2,0,1:T(8,128)S(1)} %bitcast.7) | data formatting | bytes 7372800

commit v5 on v4

--- a/solution.py
+++ b/solution.py
@@ -27,7 +27,7 @@
 def kernel(
     st, zc, df, cp, fr, bw, ti, ct, out,
     S, C, W, A, C0, R, zc_v, df_v, cp_v, fr_v, bw_v, ti_v, ct_v, ss, rs, ls,
-    from_east, from_west,
+    from_east, from_west, from_lat,
 ):
     la = lax.axis_index("lat")
     lo = lax.axis_index("lon")
@@ -45,10 +45,6 @@
 
     barrier = pltpu.get_barrier_semaphore()
 
-    def greet(*who):
-        for device in who:
-            pl.semaphore_signal(barrier, inc=1, device_id=device, device_id_type=MESH)
-
     first = lax.rem(lo, 8) == 0
     final = lax.rem(lo, 8) == 7
     middle = jnp.logical_not(first)
@@ -65,8 +61,18 @@
 
     pl.when(going)(lambda: tell(barrier, east))
     pl.when(first)(lambda: tell(barrier, west))
-    pl.when(has_up)(lambda: greet((la + 1, lo)))
-    pl.when(has_down)(lambda: greet((la - 1, lo)))
+    odd = lax.rem(la, 2) == 1
+    even = jnp.logical_not(odd)
+    beside = jnp.where(has_up, 1, 0) + jnp.where(has_down, 1, 0)
+
+    def tell_lat(semaphore):
+        def one(device):
+            pl.semaphore_signal(semaphore, inc=1, device_id=device, device_id_type=MESH)
+
+        pl.when(has_up)(lambda: one((la + 1, lo)))
+        pl.when(has_down)(lambda: one((la - 1, lo)))
+
+    pl.when(odd)(lambda: tell_lat(barrier))
 
     small = [(zc, zc_v), (df, df_v), (cp, cp_v), (fr, fr_v), (bw, bw_v), (ti, ti_v), (ct, ct_v)]
     loads = [pltpu.make_async_copy(src, dst, ls.at[i]) for i, (src, dst) in enumerate(small)]
@@ -172,17 +178,37 @@
         def _(j):
             smooth(t, HALO + jnp.minimum(j * BLOCK, m - BLOCK), BLOCK)
 
-    def edges(*tiles):
+    def edge(t, right, known):
+        place = [COLS - 1 - i if right else i for i in range(HALO)]
+        rows = pl.ds(pl.multiple_of(8 * t, 8), 8)
+        most = HALO + 2 * MAXB
+        wanted = range(HALO, most) if known else range(HALO)
+        source = {q: C[t, COLS + 2 * MAXB - 1 - q if right else q] for q in wanted}
+        total = [None if known else out[i, rows, :] for i in place]
+        for k in range(MAXB + 1):
+            weight = W[k, t]
+            for i in range(HALO):
+                reached = sorted({i + MAXB - k, i + MAXB + k})
+                values = [source[q] for q in reached if q in source]
+                if values:
+                    value = weight * (values[0] if len(values) == 1 else values[0] + values[1])
+                    total[i] = value if total[i] is None else total[i] + value
+        for i in range(HALO):
+            out[place[i], rows, :] = total[i]
+
+    def both_edges(known):
+        @pl.loop(0, TILES)
+        def _(t):
+            edge(t, False, known)
+            edge(t, True, known)
+
+    def close():
         far = COLS + MAXB - 1
-        parts = [(t, q0, HALO) for t in tiles for q0 in (0, far)]
+        parts = [(t, q0, HALO) for t in range(TILES) for q0 in (0, far)]
         value = couple(*parts)
         for i, (t, q0, size) in enumerate(parts):
             C[t, q0 : q0 + size] = value[i * size : i * size + size]
-        for t in tiles:
-
-            @pl.loop(0, 2)
-            def _(j):
-                smooth(t, j * (COLS - HALO), HALO)
+        both_edges(False)
 
     def plain(t):
         @pl.loop(0, COLS // PLAIN)
@@ -199,12 +225,11 @@
             inner(2)
 
     count = (
-        jnp.where(has_up, 1, 0)
-        + jnp.where(has_down, 1, 0)
+        jnp.where(odd, 0, beside)
         + jnp.where(first, 0, neighbours)
         + jnp.where(final, neighbours, 0)
     )
-    pl.semaphore_wait(barrier, count)
+    pl.when(count > 0)(lambda: pl.semaphore_wait(barrier, count))
 
     def send(src, dst, i, device):
         return pltpu.make_async_remote_copy(
@@ -214,15 +239,10 @@
 
     last = COLS - HALO
     high = HALO + COLS
-    wide = []
-    for t in range(TILES):
-        here, there = slice(8 * t, 8 * t + 8), slice(8 * t + 8, 8 * t + 16)
-        wide.append(
-            (
-                send(st.at[last:COLS, here], S.at[0:HALO, there], 2 * t, (la, east)),
-                send(st.at[0:HALO, here], S.at[high : high + HALO, there], 2 * t + 1, (la, west)),
-            )
-        )
+    wide = (
+        send(st.at[last:COLS], S.at[0:HALO, 8 : 8 + ROWS], 2, (la, east)),
+        send(st.at[0:HALO], S.at[high : high + HALO, 8 : 8 + ROWS], 3, (la, west)),
+    )
     thin = (
         send(st.at[COLS - 1 : COLS], S.at[HALO - 1 : HALO, 8 : 8 + ROWS], 0, (la, east)),
         send(st.at[0:1], S.at[high : high + 1, 8 : 8 + ROWS], 1, (la, west)),
@@ -250,17 +270,21 @@
     to_down = has_down & is_polar(la - 1)
 
     def start_east():
-        pl.when(polar)(lambda: start(*[pair[0] for pair in wide]))
+        pl.when(polar)(lambda: start(wide[0]))
         pl.when(jnp.logical_not(polar))(lambda: start(thin[0]))
         pl.when(to_up)(lambda: start(up_east))
         pl.when(to_down)(lambda: start(down_east))
 
     def start_west():
-        pl.when(polar)(lambda: start(*[pair[1] for pair in wide]))
+        pl.when(polar)(lambda: start(wide[1]))
         pl.when(jnp.logical_not(polar))(lambda: start(thin[1]))
         pl.when(to_up)(lambda: start(up_west))
         pl.when(to_down)(lambda: start(down_west))
 
+    def start_lat():
+        pl.when(has_up)(lambda: start(up))
+        pl.when(has_down)(lambda: start(down))
+
     @pl.when(final)
     def _():
         start_east()
@@ -271,15 +295,23 @@
         tell(from_east, west)
         start_west()
 
-    pl.when(has_up)(lambda: start(up))
-    pl.when(has_down)(lambda: start(down))
     pl.when(middle)(fetch)
+
+    @pl.when(even)
+    def _():
+        tell_lat(from_lat)
+        start_lat()
 
     @pl.when(going)
     def _():
         pl.semaphore_wait(from_east, neighbours)
         start_east()
 
+    @pl.when(odd)
+    def _():
+        pl.semaphore_wait(from_lat, beside)
+        start_lat()
+
     def clear(row):
         S[:, row : row + 1, :] = jnp.zeros((S.shape[0], 1, CH), F32)
 
@@ -300,15 +332,11 @@
     def _():
         inner(0)
         inner(3)
+        both_edges(True)
         pl.when(has_down)(lambda: wait_recv(up_east, up_west))
         pl.when(has_up)(lambda: wait_recv(down_east, down_west))
-        wait_recv(*wide[0])
-        wait_recv(*wide[1])
-        edges(0)
-        wait_recv(*wide[2])
-        edges(1)
-        wait_recv(*wide[3])
-        edges(2, 3)
+        wait_recv(*wide)
+        close()
 
     @pl.when(jnp.logical_not(polar))
     def _():
@@ -316,7 +344,7 @@
         for t in range(TILES):
             plain(t)
 
-    pl.when(polar)(lambda: wait_send(*[copy for pair in wide for copy in pair]))
+    pl.when(polar)(lambda: wait_send(*wide))
     pl.when(jnp.logical_not(polar))(lambda: wait_send(*thin))
     pl.when(has_up)(lambda: wait_send(up))
     pl.when(has_down)(lambda: wait_send(down))
@@ -352,6 +380,7 @@
             pltpu.SemaphoreType.DMA((8,)),
             pltpu.SemaphoreType.REGULAR,
             pltpu.SemaphoreType.REGULAR,
+            pltpu.SemaphoreType.REGULAR,
         ],
         compiler_params=pltpu.CompilerParams(
             collective_id=0, has_side_effects=True, vmem_limit_bytes=56 * 1024 * 1024

time: 23 us -> 21.9 us (0.952)
  Pallas kernels: 21.1 us -> 20 us
    pallas_call x1, Pallas kernels: 21.1 us -> 20 us  [local(): pl.pallas_call(kernel, out_shape=pltpu.VMEM((COLS, ROWS, CH), F32), in_sp...]
where the time goes in v5:
time: 21.9 us; the launch traced here: 21.8 us
  Pallas kernels  20 us (91%)
  local copies, waits for them, and re-layouts  1.84 us (8%)
    pallas_call x1, Pallas kernels, local(): pl.pallas_call(kernel, out_shape=pltpu.VMEM((COLS, ROWS, CH), F32), in_sp...  20 us
    unnamed x1, local copies, waits for them, and re-layouts  1.84 us

profile of v5, /device:TPU:1, one launch (start us, length us, event | category | flops | bytes accessed | tf_op | source)
XLA Modules:
  0.0 21.8 jit_solution(15926065135783331737)
XLA Ops:
  0.0 20.0 %shard_map.82 = f32[225,32,128]{2,1,0:T(8,128)S(1)} custom-call(f32[225,32,128]{2,1,0:T(8,128)} %bitcast.8, f32[1,32]{1,0:T(1,128)} %bitcast.12, f32[1,128]{1,0:T(1,128)} %bitcast.13, f32[128,128]{1,0:T(8,128)} %cp.1, s32[1,192]{1,0:T(1,128)} %bitcast.11, s32[1,512]{1,0:T(1,128)} %bitcast.9, s32[1,512]{1,0:T(1,128)} %bitcast.10, f32[16,17]{1,0:T(8,128)} %ct.1), custom_call_target="tpu_custom_call" | custom-call | tf_op jit(solution)/shard_map/pallas_call | solution.py:363
  20.0 1.8 %copy.10 = f32[32,225,128]{2,0,1:T(8,128)} copy(f32[32,225,128]{2,0,1:T(8,128)S(1)} %bitcast.7) | data formatting | bytes 7372800

commit v6 on v5

--- a/solution.py
+++ b/solution.py
@@ -12,7 +12,7 @@
 COLS = 225
 CH = 128
 TILES = ROWS // 8
-CHUNK = 112
+CHUNK = COLS - 2
 PLAIN = 75
 BLOCK = 8
 MESH = pl.DeviceIdType.MESH
@@ -40,30 +40,25 @@
     polar = is_polar(la)
     has_up = la < 15
     has_down = la > 0
-    corner_up = has_up & (polar | is_polar(la + 1))
-    corner_down = has_down & (polar | is_polar(la - 1))
 
     barrier = pltpu.get_barrier_semaphore()
 
-    first = lax.rem(lo, 8) == 0
-    final = lax.rem(lo, 8) == 7
-    middle = jnp.logical_not(first)
-    going = jnp.logical_not(final)
-    neighbours = 1 + jnp.where(corner_up, 1, 0) + jnp.where(corner_down, 1, 0)
+    place = lax.rem(lo, 8)
+    first = place == 0
+    pivot = place == 6
+    final = place == 7
+    rising = place < 6
+    inside = jnp.logical_not(first | final)
+    beside = jnp.where(has_up, 1, 0) + jnp.where(has_down, 1, 0)
+    neighbours = 1 + beside
 
     def tell(semaphore, side):
         def one(device):
             pl.semaphore_signal(semaphore, inc=1, device_id=device, device_id_type=MESH)
 
         one((la, side))
-        pl.when(corner_up)(lambda: one((la + 1, side)))
-        pl.when(corner_down)(lambda: one((la - 1, side)))
-
-    pl.when(going)(lambda: tell(barrier, east))
-    pl.when(first)(lambda: tell(barrier, west))
-    odd = lax.rem(la, 2) == 1
-    even = jnp.logical_not(odd)
-    beside = jnp.where(has_up, 1, 0) + jnp.where(has_down, 1, 0)
+        pl.when(has_up)(lambda: one((la + 1, side)))
+        pl.when(has_down)(lambda: one((la - 1, side)))
 
     def tell_lat(semaphore):
         def one(device):
@@ -72,7 +67,11 @@
         pl.when(has_up)(lambda: one((la + 1, lo)))
         pl.when(has_down)(lambda: one((la - 1, lo)))
 
-    pl.when(odd)(lambda: tell_lat(barrier))
+    odd = lax.rem(la, 2) == 1
+    even = jnp.logical_not(odd)
+    pl.when(odd & jnp.logical_not(final))(lambda: tell_lat(barrier))
+    pl.when(rising)(lambda: tell(barrier, east))
+    pl.when(first)(lambda: tell(barrier, west))
 
     small = [(zc, zc_v), (df, df_v), (cp, cp_v), (fr, fr_v), (bw, bw_v), (ti, ti_v), (ct, ct_v)]
     loads = [pltpu.make_async_copy(src, dst, ls.at[i]) for i, (src, dst) in enumerate(small)]
@@ -216,18 +215,10 @@
             i0 = j * PLAIN
             out[pl.ds(i0, PLAIN), 8 * t : 8 * t + 8, :] = couple((t, i0 + MAXB, PLAIN))
 
-    def ahead():
-        prepare()
-
-        @pl.when(polar)
-        def _():
-            inner(1)
-            inner(2)
-
     count = (
-        jnp.where(odd, 0, beside)
-        + jnp.where(first, 0, neighbours)
-        + jnp.where(final, neighbours, 0)
+        jnp.where(odd | final, 0, beside)
+        + jnp.where(inside, neighbours, 0)
+        + jnp.where(pivot | final, neighbours, 0)
     )
     pl.when(count > 0)(lambda: pl.semaphore_wait(barrier, count))
 
@@ -270,16 +261,16 @@
     to_down = has_down & is_polar(la - 1)
 
     def start_east():
+        pl.when(to_up)(lambda: start(up_east))
+        pl.when(to_down)(lambda: start(down_east))
         pl.when(polar)(lambda: start(wide[0]))
         pl.when(jnp.logical_not(polar))(lambda: start(thin[0]))
-        pl.when(to_up)(lambda: start(up_east))
-        pl.when(to_down)(lambda: start(down_east))
 
     def start_west():
+        pl.when(to_up)(lambda: start(up_west))
+        pl.when(to_down)(lambda: start(down_west))
         pl.when(polar)(lambda: start(wide[1]))
         pl.when(jnp.logical_not(polar))(lambda: start(thin[1]))
-        pl.when(to_up)(lambda: start(up_west))
-        pl.when(to_down)(lambda: start(down_west))
 
     def start_lat():
         pl.when(has_up)(lambda: start(up))
@@ -287,44 +278,57 @@
 
     @pl.when(final)
     def _():
+        tell(from_west, east)
         start_east()
-        tell(from_west, east)
-
-    @pl.when(middle)
+        tell(barrier, west)
+
+    @pl.when(inside)
     def _():
         tell(from_east, west)
+        pl.when(pivot)(lambda: tell(from_west, east))
         start_west()
 
-    pl.when(middle)(fetch)
-
-    @pl.when(even)
-    def _():
-        tell_lat(from_lat)
-        start_lat()
-
-    @pl.when(going)
+    pl.when(even & jnp.logical_not(final))(lambda: tell_lat(from_lat))
+    pl.when(pivot)(start_east)
+    pl.when(jnp.logical_not(first))(fetch)
+    pl.when(even & jnp.logical_not(final))(start_lat)
+
+    @pl.when(rising)
     def _():
         pl.semaphore_wait(from_east, neighbours)
         start_east()
 
-    @pl.when(odd)
+    @pl.when(odd & jnp.logical_not(final))
     def _():
         pl.semaphore_wait(from_lat, beside)
         start_lat()
 
+    @pl.when(final)
+    def _():
+        pl.semaphore_wait(from_west, neighbours)
+        start_west()
+
+    def answer():
+        pl.semaphore_wait(from_west, neighbours)
+        pl.semaphore_signal(from_lat, inc=1, device_id=(la, west), device_id_type=MESH)
+        start_west()
+
+    def follow():
+        pl.semaphore_wait(from_lat, 1)
+        start_lat()
+
     def clear(row):
         S[:, row : row + 1, :] = jnp.zeros((S.shape[0], 1, CH), F32)
 
     pl.when(jnp.logical_not(has_down))(lambda: clear(7))
     pl.when(jnp.logical_not(has_up))(lambda: clear(40))
 
-    ahead()
-
-    @pl.when(first)
-    def _():
-        pl.semaphore_wait(from_west, neighbours)
-        start_west()
-
+    prepare()
+    pl.when(polar)(lambda: inner(1))
+    pl.when(final)(follow)
+    pl.when(lo == 8)(answer)
+    pl.when(polar)(lambda: inner(2))
+    pl.when(lo == 0)(answer)
     pl.when(has_down)(lambda: wait_recv(up))
     pl.when(has_up)(lambda: wait_recv(down))
 

time: 21.9 us -> 19.5 us (0.89)
  Pallas kernels: 20 us -> 17.5 us
    pallas_call x1, Pallas kernels: 20 us -> 17.5 us  [local(): pl.pallas_call(kernel, out_shape=pltpu.VMEM((COLS, ROWS, CH), F32), in_sp...]
where the time goes in v6:
time: 19.5 us; the launch traced here: 19.4 us
  Pallas kernels  17.5 us (90%)
  local copies, waits for them, and re-layouts  1.84 us (9%)
    pallas_call x1, Pallas kernels, local(): pl.pallas_call(kernel, out_shape=pltpu.VMEM((COLS, ROWS, CH), F32), in_sp...  17.5 us
    unnamed x1, local copies, waits for them, and re-layouts  1.84 us

profile of v6, /device:TPU:1, one launch (start us, length us, event | category | flops | bytes accessed | tf_op | source)
XLA Modules:
  0.0 19.4 jit_solution(7898619241348819879)
XLA Ops:
  0.0 17.5 %shard_map.82 = f32[225,32,128]{2,1,0:T(8,128)S(1)} custom-call(f32[225,32,128]{2,1,0:T(8,128)} %bitcast.8, f32[1,32]{1,0:T(1,128)} %bitcast.12, f32[1,128]{1,0:T(1,128)} %bitcast.13, f32[128,128]{1,0:T(8,128)} %cp.1, s32[1,192]{1,0:T(1,128)} %bitcast.11, s32[1,512]{1,0:T(1,128)} %bitcast.9, s32[1,512]{1,0:T(1,128)} %bitcast.10, f32[16,17]{1,0:T(8,128)} %ct.1), custom_call_target="tpu_custom_call" | custom-call | tf_op jit(solution)/shard_map/pallas_call | solution.py:367
  17.5 1.8 %copy.10 = f32[32,225,128]{2,0,1:T(8,128)} copy(f32[32,225,128]{2,0,1:T(8,128)S(1)} %bitcast.7) | data formatting | bytes 7372800

commit v7 on v6

--- a/solution.py
+++ b/solution.py
@@ -78,16 +78,15 @@
     body = pltpu.make_async_copy(st, S.at[HALO : HALO + COLS, 8 : 8 + ROWS], ls.at[7])
 
     def fetch():
-        body.start()
         for load in loads:
             load.start()
+        body.start()
 
     pl.when(first)(fetch)
 
     def prepare():
         for load in loads:
             load.wait()
-        body.wait()
 
         def iota(shape, dim):
             return lax.broadcasted_iota(jnp.int32, shape, dim)
@@ -282,50 +281,48 @@
         start_east()
         tell(barrier, west)
 
+    pl.when(even & jnp.logical_not(final))(lambda: tell_lat(from_lat))
+
     @pl.when(inside)
     def _():
+        pl.when(pivot)(lambda: tell(from_west, east))
         tell(from_east, west)
-        pl.when(pivot)(lambda: tell(from_west, east))
-        start_west()
-
-    pl.when(even & jnp.logical_not(final))(lambda: tell_lat(from_lat))
+
+    pl.when(even & jnp.logical_not(final))(start_lat)
+    pl.when(inside)(start_west)
     pl.when(pivot)(start_east)
     pl.when(jnp.logical_not(first))(fetch)
-    pl.when(even & jnp.logical_not(final))(start_lat)
+
+    prepare()
+    body.wait()
+
+    @pl.when(odd & jnp.logical_not(final))
+    def _():
+        pl.semaphore_wait(from_lat, beside)
+        start_lat()
 
     @pl.when(rising)
     def _():
         pl.semaphore_wait(from_east, neighbours)
         start_east()
 
-    @pl.when(odd & jnp.logical_not(final))
-    def _():
-        pl.semaphore_wait(from_lat, beside)
+    @pl.when(final)
+    def _():
+        pl.semaphore_wait(from_west, neighbours)
         start_lat()
-
-    @pl.when(final)
-    def _():
+        start_west()
+
+    def answer():
         pl.semaphore_wait(from_west, neighbours)
         start_west()
 
-    def answer():
-        pl.semaphore_wait(from_west, neighbours)
-        pl.semaphore_signal(from_lat, inc=1, device_id=(la, west), device_id_type=MESH)
-        start_west()
-
-    def follow():
-        pl.semaphore_wait(from_lat, 1)
-        start_lat()
-
     def clear(row):
         S[:, row : row + 1, :] = jnp.zeros((S.shape[0], 1, CH), F32)
 
     pl.when(jnp.logical_not(has_down))(lambda: clear(7))
     pl.when(jnp.logical_not(has_up))(lambda: clear(40))
 
-    prepare()
     pl.when(polar)(lambda: inner(1))
-    pl.when(final)(follow)
     pl.when(lo == 8)(answer)
     pl.when(polar)(lambda: inner(2))
     pl.when(lo == 0)(answer)

time: 19.5 us -> 19.4 us (level)
  no operation moved by 1% of the time
where the time goes in v7:
time: 19.4 us
  Pallas kernels  17.5 us (90%)
  local copies, waits for them, and re-layouts  1.84 us (9%)
    pallas_call x1, Pallas kernels, local(): pl.pallas_call(kernel, out_shape=pltpu.VMEM((COLS, ROWS, CH), F32), in_sp...  17.5 us
    unnamed x1, local copies, waits for them, and re-layouts  1.84 us

profile of v7, /device:TPU:1, one launch (start us, length us, event | category | flops | bytes accessed | tf_op | source)
XLA Modules:
  0.0 19.4 jit_solution(2965381477740223805)
XLA Ops:
  0.0 17.5 %shard_map.82 = f32[225,32,128]{2,1,0:T(8,128)S(1)} custom-call(f32[225,32,128]{2,1,0:T(8,128)} %bitcast.8, f32[1,32]{1,0:T(1,128)} %bitcast.12, f32[1,128]{1,0:T(1,128)} %bitcast.13, f32[128,128]{1,0:T(8,128)} %cp.1, s32[1,192]{1,0:T(1,128)} %bitcast.11, s32[1,512]{1,0:T(1,128)} %bitcast.9, s32[1,512]{1,0:T(1,128)} %bitcast.10, f32[16,17]{1,0:T(8,128)} %ct.1), custom_call_target="tpu_custom_call" | custom-call | tf_op jit(solution)/shard_map/pallas_call | solution.py:364
  17.5 1.8 %copy.10 = f32[32,225,128]{2,0,1:T(8,128)} copy(f32[32,225,128]{2,0,1:T(8,128)S(1)} %bitcast.7) | data formatting | bytes 7372800

commit v8 on v7

--- a/solution.py
+++ b/solution.py
@@ -27,7 +27,7 @@
 def kernel(
     st, zc, df, cp, fr, bw, ti, ct, out,
     S, C, W, A, C0, R, zc_v, df_v, cp_v, fr_v, bw_v, ti_v, ct_v, ss, rs, ls,
-    from_east, from_west, from_lat,
+    from_east, from_west, from_far, from_lat,
 ):
     la = lax.axis_index("lat")
     lo = lax.axis_index("lon")
@@ -52,20 +52,19 @@
     beside = jnp.where(has_up, 1, 0) + jnp.where(has_down, 1, 0)
     neighbours = 1 + beside
 
+    def tell_one(semaphore, device):
+        pl.semaphore_signal(semaphore, inc=1, device_id=device, device_id_type=MESH)
+
+    def tell_far(semaphore, side):
+        pl.when(has_up)(lambda: tell_one(semaphore, (la + 1, side)))
+        pl.when(has_down)(lambda: tell_one(semaphore, (la - 1, side)))
+
     def tell(semaphore, side):
-        def one(device):
-            pl.semaphore_signal(semaphore, inc=1, device_id=device, device_id_type=MESH)
-
-        one((la, side))
-        pl.when(has_up)(lambda: one((la + 1, side)))
-        pl.when(has_down)(lambda: one((la - 1, side)))
+        tell_one(semaphore, (la, side))
+        tell_far(semaphore, side)
 
     def tell_lat(semaphore):
-        def one(device):
-            pl.semaphore_signal(semaphore, inc=1, device_id=device, device_id_type=MESH)
-
-        pl.when(has_up)(lambda: one((la + 1, lo)))
-        pl.when(has_down)(lambda: one((la - 1, lo)))
+        tell_far(semaphore, lo)
 
     odd = lax.rem(la, 2) == 1
     even = jnp.logical_not(odd)
@@ -200,13 +199,18 @@
             edge(t, False, known)
             edge(t, True, known)
 
-    def close():
-        far = COLS + MAXB - 1
-        parts = [(t, q0, HALO) for t in range(TILES) for q0 in (0, far)]
-        value = couple(*parts)
-        for i, (t, q0, size) in enumerate(parts):
-            C[t, q0 : q0 + size] = value[i * size : i * size + size]
-        both_edges(False)
+    def close(right):
+        pl.when(has_down)(lambda: wait_recv(up_west if right else up_east))
+        pl.when(has_up)(lambda: wait_recv(down_west if right else down_east))
+        wait_recv(wide[1] if right else wide[0])
+        q0 = COLS + MAXB - 1 if right else 0
+        value = couple(*[(t, q0, HALO) for t in range(TILES)])
+        for t in range(TILES):
+            C[t, q0 : q0 + HALO] = value[t * HALO : t * HALO + HALO]
+
+        @pl.loop(0, TILES)
+        def _(t):
+            edge(t, right, False)
 
     def plain(t):
         @pl.loop(0, COLS // PLAIN)
@@ -265,9 +269,11 @@
         pl.when(polar)(lambda: start(wide[0]))
         pl.when(jnp.logical_not(polar))(lambda: start(thin[0]))
 
-    def start_west():
+    def start_west_far():
         pl.when(to_up)(lambda: start(up_west))
         pl.when(to_down)(lambda: start(down_west))
+
+    def start_west():
         pl.when(polar)(lambda: start(wide[1]))
         pl.when(jnp.logical_not(polar))(lambda: start(thin[1]))
 
@@ -277,18 +283,24 @@
 
     @pl.when(final)
     def _():
-        tell(from_west, east)
+        tell_one(from_west, (la, east))
         start_east()
+        tell_far(from_far, east)
         tell(barrier, west)
 
     pl.when(even & jnp.logical_not(final))(lambda: tell_lat(from_lat))
 
     @pl.when(inside)
     def _():
-        pl.when(pivot)(lambda: tell(from_west, east))
         tell(from_east, west)
 
+        @pl.when(pivot)
+        def _():
+            tell_one(from_west, (la, east))
+            tell_far(from_far, east)
+
     pl.when(even & jnp.logical_not(final))(start_lat)
+    pl.when(inside)(start_west_far)
     pl.when(inside)(start_west)
     pl.when(pivot)(start_east)
     pl.when(jnp.logical_not(first))(fetch)
@@ -308,13 +320,19 @@
 
     @pl.when(final)
     def _():
-        pl.semaphore_wait(from_west, neighbours)
+        pl.semaphore_wait(from_west, 1)
         start_lat()
+        pl.semaphore_wait(from_far, beside)
+        start_west_far()
         start_west()
 
     def answer():
-        pl.semaphore_wait(from_west, neighbours)
+        pl.semaphore_wait(from_west, 1)
         start_west()
+
+    def answer_far():
+        pl.semaphore_wait(from_far, beside)
+        start_west_far()
 
     def clear(row):
         S[:, row : row + 1, :] = jnp.zeros((S.shape[0], 1, CH), F32)
@@ -332,18 +350,27 @@
     @pl.when(polar)
     def _():
         inner(0)
+        pl.when(lo == 8)(answer_far)
         inner(3)
         both_edges(True)
-        pl.when(has_down)(lambda: wait_recv(up_east, up_west))
-        pl.when(has_up)(lambda: wait_recv(down_east, down_west))
-        wait_recv(*wide)
-        close()
+        pl.when(lo == 0)(answer_far)
+
+        @pl.when(first)
+        def _():
+            close(True)
+            close(False)
+
+        @pl.when(jnp.logical_not(first))
+        def _():
+            close(False)
+            close(True)
 
     @pl.when(jnp.logical_not(polar))
     def _():
         wait_recv(*thin)
         for t in range(TILES):
             plain(t)
+        pl.when(first)(answer_far)
 
     pl.when(polar)(lambda: wait_send(*wide))
     pl.when(jnp.logical_not(polar))(lambda: wait_send(*thin))
@@ -382,6 +409,7 @@
             pltpu.SemaphoreType.REGULAR,
             pltpu.SemaphoreType.REGULAR,
             pltpu.SemaphoreType.REGULAR,
+            pltpu.SemaphoreType.REGULAR,
         ],
         compiler_params=pltpu.CompilerParams(
             collective_id=0, has_side_effects=True, vmem_limit_bytes=56 * 1024 * 1024

time: 19.4 us -> 18.7 us (0.964)
  Pallas kernels: 17.5 us -> 16.7 us
    pallas_call x1, Pallas kernels: 17.5 us -> 16.7 us  [local(): pl.pallas_call(kernel, out_shape=pltpu.VMEM((COLS, ROWS, CH), F32), in_sp...]
where the time goes in v8:
time: 18.7 us; the launch traced here: 18.6 us
  Pallas kernels  16.7 us (89%)
  local copies, waits for them, and re-layouts  1.84 us (10%)
    pallas_call x1, Pallas kernels, local(): pl.pallas_call(kernel, out_shape=pltpu.VMEM((COLS, ROWS, CH), F32), in_sp...  16.7 us
    unnamed x1, local copies, waits for them, and re-layouts  1.84 us

profile of v8, /device:TPU:1, one launch (start us, length us, event | category | flops | bytes accessed | tf_op | source)
XLA Modules:
  0.0 18.6 jit_solution(13520804240075064862)
XLA Ops:
  0.0 16.7 %shard_map.82 = f32[225,32,128]{2,1,0:T(8,128)S(1)} custom-call(f32[225,32,128]{2,1,0:T(8,128)} %bitcast.8, f32[1,32]{1,0:T(1,128)} %bitcast.12, f32[1,128]{1,0:T(1,128)} %bitcast.13, f32[128,128]{1,0:T(8,128)} %cp.1, s32[1,192]{1,0:T(1,128)} %bitcast.11, s32[1,512]{1,0:T(1,128)} %bitcast.9, s32[1,512]{1,0:T(1,128)} %bitcast.10, f32[16,17]{1,0:T(8,128)} %ct.1), custom_call_target="tpu_custom_call" | custom-call | tf_op jit(solution)/shard_map/pallas_call | solution.py:391
  16.7 1.8 %copy.10 = f32[32,225,128]{2,0,1:T(8,128)} copy(f32[32,225,128]{2,0,1:T(8,128)S(1)} %bitcast.7) | data formatting | bytes 7372800

commit v9 on v8

--- a/solution.py
+++ b/solution.py
@@ -24,9 +24,83 @@
     return [min(i * size, total - size) for i in range((total + size - 1) // size)]
 
 
+def stepped(S, A, C0, df_v, t, q0, size):
+    low = 8 + 8 * t
+    centre = S[pl.ds(q0 + 1, size), low : low + 8, :]
+    sides = S[pl.ds(q0 + 2, size), low : low + 8, :] + S[pl.ds(q0, size), low : low + 8, :]
+    poles = (
+        S[pl.ds(q0 + 1, size), low + 1 : low + 9, :] + S[pl.ds(q0 + 1, size), low - 1 : low + 7, :]
+    )
+    rows = slice(8 * t, 8 * t + 8)
+    value = (
+        C0[rows][None] * centre
+        + A[rows][None] * sides
+        + (MERIDIONAL * df_v[...])[None] * poles
+    )
+    return value.reshape(size * 8, CH)
+
+
+def coupled(S, A, C0, R, df_v, *parts):
+    flat = [stepped(S, A, C0, df_v, *part) for part in parts]
+    flat = flat[0] if len(flat) == 1 else jnp.concatenate(flat, axis=0)
+    big = flat.astype(BF16)
+    small = (flat - big.astype(F32)).astype(BF16)
+    wide = jnp.dot(jnp.concatenate([big, small], axis=1), R[...], preferred_element_type=F32)
+    flat = flat + (wide[:, :CH] + wide[:, CH:])
+    return flat.reshape(flat.shape[0] // 8, 8, CH)
+
+
+def edge(C, W, source_of, target, t, right, known):
+    place = [COLS - 1 - i if right else i for i in range(HALO)]
+    rows = pl.ds(pl.multiple_of(8 * t, 8), 8)
+    most = HALO + 2 * MAXB
+    wanted = range(HALO, most) if known else range(HALO)
+    source = {q: C[t, COLS + 2 * MAXB - 1 - q if right else q] for q in wanted}
+    total = [None if known else source_of[i, rows, :] for i in place]
+    for k in range(MAXB + 1):
+        weight = W[k, t]
+        for i in range(HALO):
+            reached = sorted({i + MAXB - k, i + MAXB + k})
+            values = [source[q] for q in reached if q in source]
+            if values:
+                value = weight * (values[0] if len(values) == 1 else values[0] + values[1])
+                total[i] = value if total[i] is None else total[i] + value
+    for i in range(HALO):
+        target[place[i], rows, :] = total[i]
+
+
+def finish(v, S, W, A, C0, R, df_v, out, C, E, sem):
+    la = lax.axis_index("lat")
+    open_edge = (lax.rem(lax.axis_index("lon"), 8) == 0) & ((la < 4) | (la >= 12))
+    inner = pltpu.make_async_copy(v.at[HALO:COLS], out.at[HALO:COLS], sem.at[0])
+    inner.start()
+
+    @pl.when(open_edge)
+    def _():
+        value = coupled(S, A, C0, R, df_v, *[(t, 0, HALO) for t in range(TILES)])
+        for t in range(TILES):
+            C[t] = value[t * HALO : t * HALO + HALO]
+
+        @pl.loop(0, TILES)
+        def _(t):
+            edge(C, W, v, E, t, False, False)
+
+        rest = pltpu.make_async_copy(E, out.at[0:HALO], sem.at[1])
+        rest.start()
+        rest.wait()
+
+    @pl.when(jnp.logical_not(open_edge))
+    def _():
+        rest = pltpu.make_async_copy(v.at[0:HALO], out.at[0:HALO], sem.at[1])
+        rest.start()
+        rest.wait()
+
+    inner.wait()
+
+
 def kernel(
-    st, zc, df, cp, fr, bw, ti, ct, out,
-    S, C, W, A, C0, R, zc_v, df_v, cp_v, fr_v, bw_v, ti_v, ct_v, ss, rs, ls,
+    st, zc, df, cp, fr, bw, ti, ct, out, S, W, A, C0, R, df_v,
+    C, zc_v, cp_v, fr_v, bw_v, ti_v, ct_v, ss, rs, ls,
     from_east, from_west, from_far, from_lat,
 ):
     la = lax.axis_index("lat")
@@ -122,33 +196,6 @@
             for k in range(taps):
                 W[k] = jnp.broadcast_to(picked[:, k : k + 1], (ROWS, CH)).reshape(TILES, 8, CH)
 
-    def stepped(t, q0, size):
-        low = 8 + 8 * t
-        centre = S[pl.ds(q0 + 1, size), low : low + 8, :]
-        sides = S[pl.ds(q0 + 2, size), low : low + 8, :] + S[pl.ds(q0, size), low : low + 8, :]
-        poles = (
-            S[pl.ds(q0 + 1, size), low + 1 : low + 9, :]
-            + S[pl.ds(q0 + 1, size), low - 1 : low + 7, :]
-        )
-        rows = slice(8 * t, 8 * t + 8)
-        value = (
-            C0[rows][None] * centre
-            + A[rows][None] * sides
-            + (MERIDIONAL * df_v[...])[None] * poles
-        )
-        return value.reshape(size * 8, CH)
-
-    def couple(*parts):
-        flat = [stepped(*part) for part in parts]
-        flat = flat[0] if len(flat) == 1 else jnp.concatenate(flat, axis=0)
-        big = flat.astype(BF16)
-        small = (flat - big.astype(F32)).astype(BF16)
-        wide = jnp.dot(
-            jnp.concatenate([big, small], axis=1), R[...], preferred_element_type=F32
-        )
-        flat = flat + (wide[:, :CH] + wide[:, CH:])
-        return flat.reshape(flat.shape[0] // 8, 8, CH)
-
     def smooth(t, i0, size):
         window = [C[t, i0 + m] for m in range(size + 2 * MAXB)]
         total = [W[0, t] * window[b + MAXB] for b in range(size)]
@@ -166,7 +213,7 @@
         @pl.loop(0, steps)
         def _(j):
             q0 = HALO + jnp.minimum(j * CHUNK, n - CHUNK)
-            C[t, pl.ds(q0, CHUNK)] = couple((t, q0, CHUNK))
+            C[t, pl.ds(q0, CHUNK)] = coupled(S, A, C0, R, df_v, (t, q0, CHUNK))
 
         m = COLS - 2 * HALO
         steps = (m + BLOCK - 1) // BLOCK
@@ -175,48 +222,33 @@
         def _(j):
             smooth(t, HALO + jnp.minimum(j * BLOCK, m - BLOCK), BLOCK)
 
-    def edge(t, right, known):
-        place = [COLS - 1 - i if right else i for i in range(HALO)]
-        rows = pl.ds(pl.multiple_of(8 * t, 8), 8)
-        most = HALO + 2 * MAXB
-        wanted = range(HALO, most) if known else range(HALO)
-        source = {q: C[t, COLS + 2 * MAXB - 1 - q if right else q] for q in wanted}
-        total = [None if known else out[i, rows, :] for i in place]
-        for k in range(MAXB + 1):
-            weight = W[k, t]
-            for i in range(HALO):
-                reached = sorted({i + MAXB - k, i + MAXB + k})
-                values = [source[q] for q in reached if q in source]
-                if values:
-                    value = weight * (values[0] if len(values) == 1 else values[0] + values[1])
-                    total[i] = value if total[i] is None else total[i] + value
-        for i in range(HALO):
-            out[place[i], rows, :] = total[i]
-
     def both_edges(known):
         @pl.loop(0, TILES)
         def _(t):
-            edge(t, False, known)
-            edge(t, True, known)
-
-    def close(right):
+            edge(C, W, out, out, t, False, known)
+            edge(C, W, out, out, t, True, known)
+
+    def arrive(right):
         pl.when(has_down)(lambda: wait_recv(up_west if right else up_east))
         pl.when(has_up)(lambda: wait_recv(down_west if right else down_east))
         wait_recv(wide[1] if right else wide[0])
+
+    def close(right):
+        arrive(right)
         q0 = COLS + MAXB - 1 if right else 0
-        value = couple(*[(t, q0, HALO) for t in range(TILES)])
+        value = coupled(S, A, C0, R, df_v, *[(t, q0, HALO) for t in range(TILES)])
         for t in range(TILES):
             C[t, q0 : q0 + HALO] = value[t * HALO : t * HALO + HALO]
 
         @pl.loop(0, TILES)
         def _(t):
-            edge(t, right, False)
+            edge(C, W, out, out, t, right, False)
 
     def plain(t):
         @pl.loop(0, COLS // PLAIN)
         def _(j):
             i0 = j * PLAIN
-            out[pl.ds(i0, PLAIN), 8 * t : 8 * t + 8, :] = couple((t, i0 + MAXB, PLAIN))
+            out[pl.ds(i0, PLAIN), 8 * t : 8 * t + 8, :] = coupled(S, A, C0, R, df_v, (t, i0 + MAXB, PLAIN))
 
     count = (
         jnp.where(odd | final, 0, beside)
@@ -263,9 +295,11 @@
     to_up = has_up & is_polar(la + 1)
     to_down = has_down & is_polar(la - 1)
 
-    def start_east():
+    def start_east_far():
         pl.when(to_up)(lambda: start(up_east))
         pl.when(to_down)(lambda: start(down_east))
+
+    def start_east():
         pl.when(polar)(lambda: start(wide[0]))
         pl.when(jnp.logical_not(polar))(lambda: start(thin[0]))
 
@@ -284,9 +318,12 @@
     @pl.when(final)
     def _():
         tell_one(from_west, (la, east))
-        start_east()
+        start_east_far()
+        late = (lo == 15) & ((la == 0) | (la == 3))
+        pl.when(jnp.logical_not(late))(start_east)
         tell_far(from_far, east)
         tell(barrier, west)
+        pl.when(late)(start_east)
 
     pl.when(even & jnp.logical_not(final))(lambda: tell_lat(from_lat))
 
@@ -302,12 +339,15 @@
     pl.when(even & jnp.logical_not(final))(start_lat)
     pl.when(inside)(start_west_far)
     pl.when(inside)(start_west)
+    pl.when(pivot)(start_east_far)
     pl.when(pivot)(start_east)
     pl.when(jnp.logical_not(first))(fetch)
 
     prepare()
     body.wait()
 
+    pl.when(polar & first)(lambda: inner(1))
+
     @pl.when(odd & jnp.logical_not(final))
     def _():
         pl.semaphore_wait(from_lat, beside)
@@ -316,6 +356,7 @@
     @pl.when(rising)
     def _():
         pl.semaphore_wait(from_east, neighbours)
+        start_east_far()
         start_east()
 
     @pl.when(final)
@@ -340,25 +381,26 @@
     pl.when(jnp.logical_not(has_down))(lambda: clear(7))
     pl.when(jnp.logical_not(has_up))(lambda: clear(40))
 
-    pl.when(polar)(lambda: inner(1))
+    pl.when(polar & jnp.logical_not(first))(lambda: inner(1))
     pl.when(lo == 8)(answer)
     pl.when(polar)(lambda: inner(2))
-    pl.when(lo == 0)(answer)
+    pl.when((lo == 0) & jnp.logical_not(polar))(answer)
     pl.when(has_down)(lambda: wait_recv(up))
     pl.when(has_up)(lambda: wait_recv(down))
 
     @pl.when(polar)
     def _():
         inner(0)
+        pl.when(lo == 0)(answer)
         pl.when(lo == 8)(answer_far)
         inner(3)
         both_edges(True)
-        pl.when(lo == 0)(answer_far)
 
         @pl.when(first)
         def _():
             close(True)
-            close(False)
+            pl.when(lo == 0)(answer_far)
+            arrive(False)
 
         @pl.when(jnp.logical_not(first))
         def _():
@@ -388,20 +430,22 @@
         turned, zonal_coef[None, :], diffusivity[None, :], coupling,
         filter_rows[None, :], band_width[None, :], table_index[None, :], coef_table,
     )
-    updated = pl.pallas_call(
+    vmem = pl.BlockSpec(memory_space=pltpu.VMEM)
+    parts = pl.pallas_call(
         kernel,
-        out_shape=pltpu.VMEM((COLS, ROWS, CH), F32),
-        in_specs=[pl.BlockSpec(memory_space=pl.ANY)] * len(args),
-        out_specs=pl.BlockSpec(memory_space=pltpu.VMEM),
-        scratch_shapes=[
+        out_shape=(
+            pltpu.VMEM((COLS, ROWS, CH), F32),
             pltpu.VMEM((COLS + 2 * HALO, ROWS + 16, CH), F32),
-            pltpu.VMEM((TILES, COLS + 2 * MAXB, 8, CH), F32),
             pltpu.VMEM((MAXB + 1, TILES, 8, CH), F32),
             pltpu.VMEM((ROWS, CH), F32),
             pltpu.VMEM((ROWS, CH), F32),
             pltpu.VMEM((2 * CH, 2 * CH), BF16),
-        ]
-        + [pltpu.VMEM(a.shape, a.dtype) for a in args[1:]]
+            pltpu.VMEM((1, CH), F32),
+        ),
+        in_specs=[pl.BlockSpec(memory_space=pltpu.HBM)] * len(args),
+        out_specs=(vmem,) * 7,
+        scratch_shapes=[pltpu.VMEM((TILES, COLS + 2 * MAXB, 8, CH), F32)]
+        + [pltpu.VMEM(args[i].shape, args[i].dtype) for i in (1, 3, 4, 5, 6, 7)]
         + [
             pltpu.SemaphoreType.DMA((14,)),
             pltpu.SemaphoreType.DMA((14,)),
@@ -412,9 +456,21 @@
             pltpu.SemaphoreType.REGULAR,
         ],
         compiler_params=pltpu.CompilerParams(
-            collective_id=0, has_side_effects=True, vmem_limit_bytes=56 * 1024 * 1024
+            collective_id=0, has_side_effects=True, vmem_limit_bytes=53 * 1024 * 1024
         ),
     )(*args)
+    updated = pl.pallas_call(
+        finish,
+        out_shape=pltpu.HBM((COLS, ROWS, CH), F32),
+        in_specs=[vmem] * 7,
+        out_specs=pl.BlockSpec(memory_space=pltpu.HBM),
+        scratch_shapes=[
+            pltpu.VMEM((TILES, HALO, 8, CH), F32),
+            pltpu.VMEM((HALO, ROWS, CH), F32),
+            pltpu.SemaphoreType.DMA((2,)),
+        ],
+        compiler_params=pltpu.CompilerParams(vmem_limit_bytes=32 * 1024 * 1024),
+    )(*parts)
     return jnp.transpose(updated, (1, 0, 2))
 
 

time: 18.7 us -> 18.2 us (0.973)
  local copies, waits for them, and re-layouts: 1.84 us -> 0 us
  Pallas kernels: 16.7 us -> 18.1 us
    unnamed x1 -> x0, local copies, waits for them, and re-layouts: 1.84 us -> none
    pallas_call x1 -> x2, Pallas kernels: 16.7 us -> 18.1 us  [the longest x1 16.2 us: local(): pl.pallas_call(kernel, out_shape=(pltpu.VMEM((COLS, ROWS, CH), F32), pltp...]
where the time goes in v9:
time: 18.2 us; the launch traced here: 18.1 us
  Pallas kernels  18.1 us (99%)
    pallas_call x1, Pallas kernels, local(): pl.pallas_call(kernel, out_shape=(pltpu.VMEM((COLS, ROWS, CH), F32), pltp...  16.2 us
    pallas_call x1, Pallas kernels, local(): pl.pallas_call(finish, out_shape=pltpu.HBM((COLS, ROWS, CH), F32), in_spe...  1.85 us

profile of v9, /device:TPU:1, one launch (start us, length us, event | category | flops | bytes accessed | tf_op | source)
XLA Modules:
  0.0 18.1 jit_solution(9721492214318577940)
XLA Ops:
  0.0 16.2 %shard_map.82 = (f32[225,32,128]{2,1,0:T(8,128)S(1)}, f32[259,48,128]{2,1,0:T(8,128)S(1)}, f32[17,4,8,128]{3,2,1,0:T(8,128)S(1)}, f32[32,128]{1,0:T(8,128)S(1)},...) custom-call(f32[225,32,128]{2,1,0:T(8,128)} %bitcast.7, f32[1,32]{1,0:T(1,128)} %bitcast.11, ...), custom_call_target="tpu_custom_call" | custom-call | tf_op jit(solution)/shard_map/pallas_call | solution.py:434
  16.2 1.9 %shard_map.83 = f32[225,32,128]{2,1,0:T(8,128)} custom-call(f32[225,32,128]{2,1,0:T(8,128)S(1)} %get-tuple-element.12.v, f32[259,48,128]{2,1,0:T(8,128)S(1)} %get-tuple-element.13.S, f32[17,4,8,128]{3,2,1,0:T(8,128)S(1)} %get-tuple-element.14.W, f32[32,128]{1,0:T(8,128)S(1)} %get-tuple-element.15.A, f32[32,128]{1,0:T(8,128)S(1)} %get-tuple-element.16.C0, ...), custom_call_target="tpu_custom_call" | custom-call | tf_op jit(solution)/shard_map/pallas_call | solution.py:462

commit v10 on v9

--- a/solution.py
+++ b/solution.py
@@ -48,6 +48,22 @@
     wide = jnp.dot(jnp.concatenate([big, small], axis=1), R[...], preferred_element_type=F32)
     flat = flat + (wide[:, :CH] + wide[:, CH:])
     return flat.reshape(flat.shape[0] // 8, 8, CH)
+
+
+class Moved:
+    def __init__(self, ref, shift):
+        self.ref, self.shift = ref, shift
+
+    def at(self, index):
+        if self.ref.ndim == 4:
+            return (index[0], index[1] + self.shift)
+        return (index[0] + self.shift,) + index[1:]
+
+    def __getitem__(self, index):
+        return self.ref[self.at(index)]
+
+    def __setitem__(self, index, value):
+        self.ref[self.at(index)] = value
 
 
 def edge(C, W, source_of, target, t, right, known):
@@ -71,29 +87,37 @@
 
 def finish(v, S, W, A, C0, R, df_v, out, C, E, sem):
     la = lax.axis_index("lat")
-    open_edge = (lax.rem(lax.axis_index("lon"), 8) == 0) & ((la < 4) | (la >= 12))
-    inner = pltpu.make_async_copy(v.at[HALO:COLS], out.at[HALO:COLS], sem.at[0])
+    polar = (la < 4) | (la >= 12)
+    high = COLS - HALO
+    inner = pltpu.make_async_copy(v.at[HALO:high], out.at[HALO:high], sem.at[0])
     inner.start()
 
-    @pl.when(open_edge)
-    def _():
-        value = coupled(S, A, C0, R, df_v, *[(t, 0, HALO) for t in range(TILES)])
-        for t in range(TILES):
-            C[t] = value[t * HALO : t * HALO + HALO]
+    def write(low, high):
+        left = pltpu.make_async_copy(low, out.at[0:HALO], sem.at[1])
+        right = pltpu.make_async_copy(high, out.at[COLS - HALO : COLS], sem.at[2])
+        left.start()
+        right.start()
+        left.wait()
+        right.wait()
+
+    @pl.when(polar)
+    def _():
+        far = COLS + MAXB - 1
+        parts = [(t, q0, HALO) for t in range(TILES) for q0 in (0, far)]
+        value = coupled(S, A, C0, R, df_v, *parts)
+        for i, (t, q0, size) in enumerate(parts):
+            C[t, (i % 2) * size : (i % 2) * size + size] = value[i * size : i * size + size]
 
         @pl.loop(0, TILES)
         def _(t):
-            edge(C, W, v, E, t, False, False)
-
-        rest = pltpu.make_async_copy(E, out.at[0:HALO], sem.at[1])
-        rest.start()
-        rest.wait()
-
-    @pl.when(jnp.logical_not(open_edge))
-    def _():
-        rest = pltpu.make_async_copy(v.at[0:HALO], out.at[0:HALO], sem.at[1])
-        rest.start()
-        rest.wait()
+            edge(Moved(C, 0), W, v, Moved(E, 0), t, False, False)
+            edge(Moved(C, HALO - far), W, v, Moved(E, HALO - high), t, True, False)
+
+        write(E.at[0:HALO], E.at[HALO : 2 * HALO])
+
+    @pl.when(jnp.logical_not(polar))
+    def _():
+        write(v.at[0:HALO], v.at[high:COLS])
 
     inner.wait()
 
@@ -233,17 +257,6 @@
         pl.when(has_up)(lambda: wait_recv(down_west if right else down_east))
         wait_recv(wide[1] if right else wide[0])
 
-    def close(right):
-        arrive(right)
-        q0 = COLS + MAXB - 1 if right else 0
-        value = coupled(S, A, C0, R, df_v, *[(t, q0, HALO) for t in range(TILES)])
-        for t in range(TILES):
-            C[t, q0 : q0 + HALO] = value[t * HALO : t * HALO + HALO]
-
-        @pl.loop(0, TILES)
-        def _(t):
-            edge(C, W, out, out, t, right, False)
-
     def plain(t):
         @pl.loop(0, COLS // PLAIN)
         def _(j):
@@ -396,16 +409,9 @@
         inner(3)
         both_edges(True)
 
-        @pl.when(first)
-        def _():
-            close(True)
-            pl.when(lo == 0)(answer_far)
-            arrive(False)
-
-        @pl.when(jnp.logical_not(first))
-        def _():
-            close(False)
-            close(True)
+        arrive(True)
+        pl.when(lo == 0)(answer_far)
+        arrive(False)
 
     @pl.when(jnp.logical_not(polar))
     def _():
@@ -465,9 +471,9 @@
         in_specs=[vmem] * 7,
         out_specs=pl.BlockSpec(memory_space=pltpu.HBM),
         scratch_shapes=[
-            pltpu.VMEM((TILES, HALO, 8, CH), F32),
-            pltpu.VMEM((HALO, ROWS, CH), F32),
-            pltpu.SemaphoreType.DMA((2,)),
+            pltpu.VMEM((TILES, 2 * HALO, 8, CH), F32),
+            pltpu.VMEM((2 * HALO, ROWS, CH), F32),
+            pltpu.SemaphoreType.DMA((3,)),
         ],
         compiler_params=pltpu.CompilerParams(vmem_limit_bytes=32 * 1024 * 1024),
     )(*parts)

time: 18.2 us -> 18.2 us (level)
  no operation moved by 1% of the time
where the time goes in v10:
time: 18.2 us; the launch traced here: 18.1 us
  Pallas kernels  18.1 us (99%)
    pallas_call x1, Pallas kernels, local(): pl.pallas_call(kernel, out_shape=(pltpu.VMEM((COLS, ROWS, CH), F32), pltp...  16.2 us
    pallas_call x1, Pallas kernels, local(): pl.pallas_call(finish, out_shape=pltpu.HBM((COLS, ROWS, CH), F32), in_spe...  1.86 us

profile of v10, /device:TPU:1, one launch (start us, length us, event | category | flops | bytes accessed | tf_op | source)
XLA Modules:
  0.0 18.1 jit_solution(12448026087548843736)
XLA Ops:
  0.0 16.2 %shard_map.82 = (f32[225,32,128]{2,1,0:T(8,128)S(1)}, f32[259,48,128]{2,1,0:T(8,128)S(1)}, f32[17,4,8,128]{3,2,1,0:T(8,128)S(1)}, f32[32,128]{1,0:T(8,128)S(1)},...) custom-call(f32[225,32,128]{2,1,0:T(8,128)} %bitcast.7, f32[1,32]{1,0:T(1,128)} %bitcast.11, ...), custom_call_target="tpu_custom_call" | custom-call | tf_op jit(solution)/shard_map/pallas_call | solution.py:440
  16.2 1.9 %shard_map.83 = f32[225,32,128]{2,1,0:T(8,128)} custom-call(f32[225,32,128]{2,1,0:T(8,128)S(1)} %get-tuple-element.12.v, f32[259,48,128]{2,1,0:T(8,128)S(1)} %get-tuple-element.13.S, f32[17,4,8,128]{3,2,1,0:T(8,128)S(1)} %get-tuple-element.14.W, f32[32,128]{1,0:T(8,128)S(1)} %get-tuple-element.15.A, f32[32,128]{1,0:T(8,128)S(1)} %get-tuple-element.16.C0, ...), custom_call_target="tpu_custom_call" | custom-call | tf_op jit(solution)/shard_map/pallas_call | solution.py:468

commit v11 on v10

--- a/solution.py
+++ b/solution.py
@@ -331,10 +331,11 @@
     @pl.when(final)
     def _():
         tell_one(from_west, (la, east))
-        start_east_far()
+        swift = la == 1
+        pl.when(jnp.logical_not(swift))(start_east_far)
         late = (lo == 15) & ((la == 0) | (la == 3))
         pl.when(jnp.logical_not(late))(start_east)
-        tell_far(from_far, east)
+        pl.when(swift)(start_east_far)
         tell(barrier, west)
         pl.when(late)(start_east)
 
@@ -382,6 +383,7 @@
 
     def answer():
         pl.semaphore_wait(from_west, 1)
+        tell_lat(from_far)
         start_west()
 
     def answer_far():
@@ -409,8 +411,8 @@
         inner(3)
         both_edges(True)
 
+        pl.when(lo == 0)(answer_far)
         arrive(True)
-        pl.when(lo == 0)(answer_far)
         arrive(False)
 
     @pl.when(jnp.logical_not(polar))

time: 18.2 us -> 17.9 us (0.984)
  Pallas kernels: 18.1 us -> 17.7 us
    pallas_call x1, Pallas kernels: 16.2 us -> 15.8 us  [local(): pl.pallas_call(kernel, out_shape=(pltpu.VMEM((COLS, ROWS, CH), F32), pltp...]
where the time goes in v11:
time: 17.9 us; the launch traced here: 17.7 us
  Pallas kernels  17.7 us (99%)
    pallas_call x1, Pallas kernels, local(): pl.pallas_call(kernel, out_shape=(pltpu.VMEM((COLS, ROWS, CH), F32), pltp...  15.8 us
    pallas_call x1, Pallas kernels, local(): pl.pallas_call(finish, out_shape=pltpu.HBM((COLS, ROWS, CH), F32), in_spe...  1.86 us

profile of v11, /device:TPU:1, one launch (start us, length us, event | category | flops | bytes accessed | tf_op | source)
XLA Modules:
  0.0 17.7 jit_solution(9202679284208619999)
XLA Ops:
  0.0 15.8 %shard_map.82 = (f32[225,32,128]{2,1,0:T(8,128)S(1)}, f32[259,48,128]{2,1,0:T(8,128)S(1)}, f32[17,4,8,128]{3,2,1,0:T(8,128)S(1)}, f32[32,128]{1,0:T(8,128)S(1)},...) custom-call(f32[225,32,128]{2,1,0:T(8,128)} %bitcast.7, f32[1,32]{1,0:T(1,128)} %bitcast.11, ...), custom_call_target="tpu_custom_call" | custom-call | tf_op jit(solution)/shard_map/pallas_call | solution.py:442
  15.8 1.9 %shard_map.83 = f32[225,32,128]{2,1,0:T(8,128)} custom-call(f32[225,32,128]{2,1,0:T(8,128)S(1)} %get-tuple-element.12.v, f32[259,48,128]{2,1,0:T(8,128)S(1)} %get-tuple-element.13.S, f32[17,4,8,128]{3,2,1,0:T(8,128)S(1)} %get-tuple-element.14.W, f32[32,128]{1,0:T(8,128)S(1)} %get-tuple-element.15.A, f32[32,128]{1,0:T(8,128)S(1)} %get-tuple-element.16.C0, ...), custom_call_target="tpu_custom_call" | custom-call | tf_op jit(solution)/shard_map/pallas_call | solution.py:470
